TPU v7x, 32 devices: a whole 2x2x4 slice. The times are simulated.
32 devices in a mesh: graph: 8 (over y, x, core), row: 4 (over z).
Axes of the slice: x: 2, y: 2, z: 4, core: 2. Of those that a mesh axis runs over, the one named last changes fastest.
Arguments:
- features: bfloat16 [24, 1024, 1024], P('graph', 'row'), may hold values from -6 to 6
- adjacency: int32 [24, 1024, 1024], P('graph', 'row'), may hold values 0 or 1
- counts: int32 [24], P('graph'), may hold values from 341 to 1024, as said below
- proj_weight: bfloat16 [1024, 1024], replicated, may hold values from -0.75 to 0.75
- skip_weight: bfloat16 [1024, 1024], replicated, may hold values from -0.1875 to 0.1875
- attn_dst: bfloat16 [4, 256], replicated, may hold values from -0.09375 to 0.09375
- attn_src: bfloat16 [4, 256], replicated, may hold values from -0.09375 to 0.09375
- attn_bias: float32 [1024], replicated, may hold values from -3 to 3
- norm_gain: float32 [1024], replicated, may hold values from 0.1 to 1.9
- norm_shift: float32 [1024], replicated, may hold values from -3 to 3
- cotangent: bfloat16 [24, 1024, 1024], P('graph', 'row'), may hold values from -6 to 6
Outputs:
- output: bfloat16 [24, 1024, 1024], P('graph', 'row')
- input_grad: bfloat16 [24, 1024, 1024], P('graph', 'row')
- proj_grad: float32 [1024, 1024], replicated
- skip_grad: float32 [1024, 1024], replicated
- attn_dst_grad: float32 [4, 256], replicated
- attn_src_grad: float32 [4, 256], replicated
- bias_grad: float32 [1024], replicated
- gain_grad: float32 [1024], replicated
- shift_grad: float32 [1024], replicated
Inputs may be any that keep to these rules, and one draw needn't show every extreme that they name: Real nodes come first in each graph; the counts rise over the graphs with some jitter, and among graphs 3k to 3k+2, for each k, at least one has all 1024 nodes real.
All inputs are finite; a program needn't handle non-finite values. No bound on the sum of `adjacency` on one device may be relied on, other than what follows from the above.
Results may differ from a plain program's by a relative error of at most 0.0087.
Values may be sent and summed in bfloat16 or wider, within the bound.
A program may use at most 192 MiB of HBM per device.

v0:
```python
import jax
import jax.numpy as jnp
from jax import lax
from jax.sharding import PartitionSpec as P

EPSILON = 1e-05


def smooth_leaky(value):
    return 0.2 * value + 0.8 * jax.nn.softplus(value)


def shards(
    features,
    adjacency,
    counts,
    proj_weight,
    skip_weight,
    attn_dst,
    attn_src,
    attn_bias,
    norm_gain,
    norm_shift,
    cotangent,
):
    graph_count, row_count, width_in = features.shape
    node_total = adjacency.shape[2]
    head_count, head_width = attn_dst.shape
    width = head_count * head_width
    row_ids = lax.axis_index("row") * row_count + jnp.arange(row_count)
    node_ids = jnp.arange(node_total)
    live_own = (row_ids[None, :] < counts[:, None]).astype(jnp.float32)
    live_all = (node_ids[None, :] < counts[:, None]).astype(jnp.float32)
    hidden = jnp.einsum(
        "grf,fd->grd", features, proj_weight, preferred_element_type=jnp.float32
    ).astype(jnp.bfloat16)
    skip_out = jnp.einsum("grf,fd->grd", features, skip_weight, preferred_element_type=jnp.float32)
    gathered = lax.all_gather(hidden, "row", axis=1, tiled=True)
    own_heads = hidden.reshape(graph_count, row_count, head_count, head_width)
    dst_score = jnp.einsum("grhc,hc->grh", own_heads, attn_dst, preferred_element_type=jnp.float32)
    src_score = jnp.einsum(
        "gnhc,hc->gnh",
        gathered.reshape(graph_count, node_total, head_count, head_width),
        attn_src,
        preferred_element_type=jnp.float32,
    )

    def logits_of(adjacent, dst_one, src_one, live_row, live_col, ids_row, ids_col):
        allowed = (
            ((adjacent > 0) | (ids_row[:, None] == ids_col[None, :]))
            & (live_row[:, None] > 0)
            & (live_col[None, :] > 0)
        )
        raw_logit = dst_one.T[:, :, None] + src_one.T[:, None, :]
        return (raw_logit, smooth_leaky(raw_logit), allowed)

    def attend(inputs):
        adjacent, dst_one, src_one, live_row, live_col, source = inputs
        raw_logit, logit, allowed = logits_of(
            adjacent, dst_one, src_one, live_row, live_col, row_ids, node_ids
        )
        peak_logit = jnp.max(jnp.where(allowed[None], logit, -1e30), axis=2)
        peak_logit = jnp.where(live_row[None, :] > 0, peak_logit, 0.0)
        weight = jnp.where(allowed[None], jnp.exp(logit - peak_logit[:, :, None]), 0.0)
        totals = jnp.sum(weight, axis=2) + (1.0 - live_row)[None, :]
        shares = (weight / totals[:, :, None]).astype(jnp.bfloat16)
        mixture = jnp.einsum(
            "hrn,nhc->rhc",
            shares,
            source.reshape(node_total, head_count, head_width),
            preferred_element_type=jnp.float32,
        )
        return (mixture.reshape(row_count, width), peak_logit, totals)

    mixture, peaks, totals_all = lax.map(
        attend, (adjacency, dst_score, src_score, live_own, live_all, gathered)
    )
    pre_act = mixture + attn_bias + skip_out
    activation = jax.nn.elu(pre_act)
    live_col3 = live_own[:, :, None]
    count_local = jnp.sum(live_own)
    sum_local = jnp.sum(activation * live_col3, axis=(0, 1))
    real_count, total_sum = lax.psum((count_local, sum_local), ("graph", "row"))
    mean_act = total_sum / real_count
    centered = activation - mean_act
    variance = (
        lax.psum(jnp.sum(centered * centered * live_col3, axis=(0, 1)), ("graph", "row"))
        / real_count
    )
    inv_std = lax.rsqrt(variance + EPSILON)
    normed = centered * inv_std
    output = ((norm_gain * normed + norm_shift) * live_col3).astype(jnp.bfloat16)
    grad_out = cotangent.astype(jnp.float32) * live_col3
    shift_grad, gain_grad = lax.psum(
        (jnp.sum(grad_out, axis=(0, 1)), jnp.sum(grad_out * normed, axis=(0, 1))), ("graph", "row")
    )
    grad_act = (
        norm_gain
        * inv_std
        * (grad_out - shift_grad / real_count - normed * gain_grad / real_count)
        * live_col3
    )
    grad_pre = grad_act * jnp.where(pre_act > 0, 1.0, jnp.exp(jnp.minimum(pre_act, 0.0)))
    grad_low = grad_pre.astype(jnp.bfloat16)

    def back_core(
        adjacent, dst_one, src_one, live_row, live_col, source, peak_logit, totals, grad_mix
    ):
        raw_logit, logit, allowed = logits_of(
            adjacent, dst_one, src_one, live_row, live_col, row_ids, node_ids
        )
        weight = jnp.where(allowed[None], jnp.exp(logit - peak_logit[:, :, None]), 0.0)
        exact_shares = weight / totals[:, :, None]
        src_heads = source.reshape(node_total, head_count, head_width)
        grad_heads = grad_mix.reshape(row_count, head_count, head_width)
        grad_shares = jnp.einsum(
            "rhc,nhc->hrn", grad_heads, src_heads, preferred_element_type=jnp.float32
        )
        spread = jnp.sum(exact_shares * grad_shares, axis=2, keepdims=True)
        grad_raw = exact_shares * (grad_shares - spread) * (0.2 + 0.8 * jax.nn.sigmoid(raw_logit))
        return (exact_shares, grad_raw, spread[:, :, 0], grad_heads)

    def attend_back(inputs):
        exact_shares, grad_raw, spread, grad_heads = back_core(*inputs)
        dst_part = jnp.sum(grad_raw, axis=2).T
        src_part = jnp.sum(grad_raw, axis=1).T
        source_part = jnp.einsum(
            "hrn,rhc->nhc",
            exact_shares.astype(jnp.bfloat16),
            grad_heads,
            preferred_element_type=jnp.float32,
        )
        return (source_part.reshape(node_total, width), src_part, dst_part)

    back_inputs = (
        adjacency,
        dst_score,
        src_score,
        live_own,
        live_all,
        gathered,
        peaks,
        totals_all,
        grad_low,
    )
    source_grad, src_grad, dst_grad = lax.map(attend_back, back_inputs)
    own_source, own_src = (
        lax.psum_scatter(source_grad, "row", scatter_dimension=1, tiled=True),
        lax.psum_scatter(src_grad, "row", scatter_dimension=1, tiled=True),
    )
    score_terms = dst_grad[..., None] * attn_dst.astype(jnp.float32) + own_src[
        ..., None
    ] * attn_src.astype(jnp.float32)
    hidden_grad = own_source + score_terms.reshape(graph_count, row_count, width)
    hidden_low = hidden_grad.astype(jnp.bfloat16)
    own_float = own_heads.astype(jnp.float32)
    dst_local = jnp.einsum("grh,grhc->hc", dst_grad, own_float, precision=lax.Precision.HIGHEST)
    src_local = jnp.einsum("grh,grhc->hc", own_src, own_float, precision=lax.Precision.HIGHEST)
    bias_local = jnp.sum(grad_pre, axis=(0, 1))
    proj_local = jnp.einsum("grf,grd->fd", features, hidden_low, preferred_element_type=jnp.float32)
    skip_local = jnp.einsum("grf,grd->fd", features, grad_low, preferred_element_type=jnp.float32)
    input_grad = (
        jnp.einsum("grd,fd->grf", hidden_low, proj_weight, preferred_element_type=jnp.float32)
        + jnp.einsum("grd,fd->grf", grad_low, skip_weight, preferred_element_type=jnp.float32)
    ).astype(jnp.bfloat16)
    proj_grad, skip_grad, dst_total, src_total, bias_grad = lax.psum(
        (proj_local, skip_local, dst_local, src_local, bias_local), ("graph", "row")
    )
    return (
        output,
        input_grad,
        proj_grad,
        skip_grad,
        dst_total,
        src_total,
        bias_grad,
        gain_grad,
        shift_grad,
    )


def solution(mesh):
    placed = (
        P("graph", "row", None),
        P("graph", "row", None),
        P("graph"),
        P(),
        P(),
        P(),
        P(),
        P(),
        P(),
        P(),
        P("graph", "row", None),
    )
    return jax.shard_map(
        shards,
        mesh=mesh,
        in_specs=placed,
        out_specs=(
            P("graph", "row", None),
            P("graph", "row", None),
            P(),
            P(),
            P(),
            P(),
            P(),
            P(),
            P(),
        ),
        check_vma=False,
    )
```

profile of v0, /device:TPU:0, one launch (start us, length us, event | category | flops | bytes accessed | tf_op | source)
XLA Modules:
  0.0 869.1 jit_solution(14679252562108573110)
XLA Ops:
  7.2 5.1 fusion.80
  15.3 115.3 %all-gather.2.cloned.1.call-done = bf16[3,1024,1024]{2,1,0:T(8,128)(2,1)} async-done(((bf16[3,256,1024]{2,1,0:T(8,128)(2,1)}), bf16[3,1024,1024]{2,1,0:T(8,128)(2,1)}) %all-gather.2.cloned.1.call-update) | async-done | bytes 6291472 | tf_op jit(solution)/shard_map/all_gather | solution.py:38
  135.2 9.2 %copy.43 = bf16[3,1024,1024]{1,2,0:T(8,128)(2,1)} copy(bf16[3,1024,1024]{2,1,0:T(8,128)(2,1)} %all-gather.2.cloned.1.call-done) | data formatting | bytes 12582912
  144.4 56.8 %while.32 = (s32[]{:T(128)}, f32[3,256,1024]{2,1,0:T(8,128)}, f32[3,4,256]{2,1,0:T(4,128)S(1)}, f32[3,4,256]{2,1,0:T(4,128)S(1)}, bf16[3,1024,1024]{1,2,0:T(8,12...) while((s32[]{:T(128)}, f32[3,256,1024]{2,1,0:T(8,128)}, ...), condition=%wide.region_3.4_spmd.clone.clone, body=%wide.region_0.3_spmd.clone.sunk.clone | while | flops 579079936 | bytes 13802385 | solution.py:75
  155.3 5.4 fusion.156
  174.2 5.4 fusion.156
  193.2 5.4 fusion.156
  208.8 38.8 %all-reduce.2 = (f32[1024]{0:T(1024)S(1)}, f32[]{:T(128)}) all-reduce(f32[1024]{0:T(1024)S(1)} %multiply_reduce_fusion.3, f32[]{:T(128)} %fusion.102), channel_id=1, replica_groups=mesh['graph'=8,'row'=4] {'graph','row'}, use_global_device_ids=true, to_apply=%region_5.6 | all-reduce | flops 1025 | bytes 8200 | tf_op jit(solution)/shard_map/psum | solution.py:83
  252.0 41.2 %psum.72 = f32[1024]{0:T(1024)S(1)} all-reduce(f32[1024]{0:T(1024)S(1)} %multiply_reduce_fusion.2), channel_id=1, replica_groups=mesh['graph'=8,'row'=4] {'graph','row'}, use_global_device_ids=true, to_apply=%region_9.10 | all-reduce | flops 1024 | bytes 8192 | tf_op jit(solution)/shard_map/psum | solution.py:87
  298.3 39.5 %all-reduce.1 = (f32[1024]{0:T(1024)S(1)}, f32[1024]{0:T(1024)S(1)}) all-reduce(f32[1024]{0:T(1024)S(1)} %get-tuple-element.321, f32[1024]{0:T(1024)S(1)} %get-tuple-element.320), channel_id=1, replica_groups=mesh['graph'=8,'row'=4] {'graph','row'}, use_global_device_ids=true, to_apply=%region_13.14 | all-reduce | flops 2048 | bytes 16384 | tf_op jit(solution)/shard_map/psum | solution.py:94
  338.5 7.5 fusion.104
  345.9 76.9 %while.33 = (s32[]{:T(128)}, f32[3,1024,1024]{1,2,0:T(8,128)}, f32[3,1024,4]{1,2,0:T(4,128)}, f32[3,256,4]{1,2,0:T(4,128)S(1)}, bf16[3,256,1024]{2,1,0:T(8,128)(...) while((s32[]{:T(128)}, f32[3,1024,1024]{1,2,0:T(8,128)}, ...), condition=%wide.region_18.19_spmd.clone.clone, body=%wide.region_14.18_spmd.clone.sunk.clone | while | flops 1665399296 | bytes 24042156 | solution.py:146
  358.6 12.4 %fusion.167 = (f32[4,256]{1,0:T(4,128)S(1)}, f32[4,1024]{1,0:T(4,128)S(1)}) fusion(f32[4,256]{1,0:T(4,128)S(1)} %get-tuple-element.602, f32[4,256]{1,0:T(4,128)S(1)} %get-tuple-element.603, f32[4,1024]{1,0:T(4,128)S(1)} %dynamic-slice_bitcast_fusion.19, f32[4,256]{1,0:T(4,128)S(1)} %dynamic-slice_bitcast_fusion.20, ...), kind=kOutput, calls=%fused_computation.159.clone.1.clone | convolution fusion | flops 1112536064 | bytes 2932736 | tf_op jit(solution)/shard_map/while/body/eval_jaxpr/sub | solution.py:120
  384.2 12.4 %fusion.167 = (f32[4,256]{1,0:T(4,128)S(1)}, f32[4,1024]{1,0:T(4,128)S(1)}) fusion(f32[4,256]{1,0:T(4,128)S(1)} %get-tuple-element.602, f32[4,256]{1,0:T(4,128)S(1)} %get-tuple-element.603, f32[4,1024]{1,0:T(4,128)S(1)} %dynamic-slice_bitcast_fusion.19, f32[4,256]{1,0:T(4,128)S(1)} %dynamic-slice_bitcast_fusion.20, ...), kind=kOutput, calls=%fused_computation.159.clone.1.clone | convolution fusion | flops 1112536064 | bytes 2932736 | tf_op jit(solution)/shard_map/while/body/eval_jaxpr/sub | solution.py:120
  409.8 12.4 %fusion.167 = (f32[4,256]{1,0:T(4,128)S(1)}, f32[4,1024]{1,0:T(4,128)S(1)}) fusion(f32[4,256]{1,0:T(4,128)S(1)} %get-tuple-element.602, f32[4,256]{1,0:T(4,128)S(1)} %get-tuple-element.603, f32[4,1024]{1,0:T(4,128)S(1)} %dynamic-slice_bitcast_fusion.19, f32[4,256]{1,0:T(4,128)S(1)} %dynamic-slice_bitcast_fusion.20, ...), kind=kOutput, calls=%fused_computation.159.clone.1.clone | convolution fusion | flops 1112536064 | bytes 2932736 | tf_op jit(solution)/shard_map/while/body/eval_jaxpr/sub | solution.py:120
  429.8 5.7 convolution_bitcast_fusion
  435.5 14.7 %reduce-scatter.7.cloned.1.call-done = f32[256,12]{1,0:T(8,128)} async-done(((f32[1024,12]{1,0:T(8,128)}), f32[256,12]{1,0:T(8,128)}) %reduce-scatter.7.cloned.1.call-update) | async-done | bytes 12304
  451.5 211.3 %reduce-scatter.5.cloned.1.call-done = f32[3,256,1024]{1,2,0:T(8,128)} async-done(((f32[3,1024,1024]{1,2,0:T(8,128)}), f32[3,256,1024]{1,2,0:T(8,128)}) %reduce-scatter.5.cloned.1.call-update) | async-done | bytes 3145744 | tf_op jit(solution)/shard_map/reduce_scatter | solution.py:148
  672.5 5.3 fusion.72
  678.5 43.4 %all-reduce = (f32[4,256]{1,0:T(4,128)}, f32[4,256]{1,0:T(4,128)}, f32[1024]{0:T(1024)}) all-reduce(f32[4,256]{1,0:T(4,128)S(1)} %get-tuple-element.393, f32[4,256]{1,0:T(4,128)S(1)} %get-tuple-element.392, f32[1024]{0:T(1024)S(1)} %copy-done.4), channel_id=1, replica_groups=mesh['graph'=8,'row'=4] {'graph','row'}, use_global_device_ids=true, to_apply=%region_23.24 | all-reduce | flops 3072 | bytes 24576 | tf_op jit(solution)/shard_map/psum | solution.py:166
  722.0 6.0 add_convert_fusion
  728.0 123.7 %all-reduce.6.cloned.1.call-done = (f32[1024,1024]{0,1:T(8,128)}, f32[1024,1024]{0,1:T(8,128)}) async-done(((f32[1024,1024]{0,1:T(8,128)}, f32[1024,1024]{0,1:T(8,128)}), (f32[1024,1024]{0,1:T(8,128)}, f32[1024,1024]{0,1:T(8,128)})) %all-reduce.6.cloned.1.call-update) | async-done | bytes 8388624 | tf_op jit(solution)/shard_map/psum | solution.py:166
  851.7 5.3 copy.49
  857.0 5.3 copy.50
  (161 shorter events, 123.2 us)
Async XLA Ops:
  7.2 194.0 %copy-start = (bf16[1024,1024]{1,0:T(8,128)(2,1)S(1)}, bf16[1024,1024]{1,0:T(8,128)(2,1)}, u32[]{:S(2)}) copy-start(bf16[1024,1024]{1,0:T(8,128)(2,1)} %param.19) | copy-start | bytes 6291460
  7.2 5.3 copy-start.10
  7.2 123.4 %all-gather.2.cloned.1.call-start = ((), (), s32[]{:S(2)}) async-start(), calls=%async_computation.2 | async-start | bytes 7864320 | tf_op jit(solution)/shard_map/all_gather | solution.py:38
  12.4 2.1 copy-start.6
  12.4 118.2 %copy-start.12 = (bf16[4,256]{1,0:T(4,128)(2,1)S(1)}, bf16[4,256]{1,0:T(4,128)(2,1)}, u32[]{:S(2)}) copy-start(bf16[4,256]{1,0:T(4,128)(2,1)} %param.21) | copy-start | bytes 6148
  12.4 437.8 %reduce-scatter.7.cloned.1.call-start = ((), (), s32[]{:S(2)}) async-start(), calls=%async_computation.4 | async-start | bytes 655360
  144.4 56.8 %copy-start.15 = (f32[1024]{0:T(1024)S(1)}, f32[1024]{0:T(1024)}, u32[]{:S(2)}) copy-start(f32[1024]{0:T(1024)} %param.22) | copy-start | bytes 12292
  205.6 1.7 copy-start.1
  207.3 85.9 %copy-start.5 = (f32[1024]{0:T(1024)S(1)}, f32[1024]{0:T(1024)}, u32[]{:S(2)}) copy-start(f32[1024]{0:T(1024)} %param.23) | copy-start | bytes 12292
  252.0 86.5 %copy-start.7 = (f32[1024]{0:T(1024)S(1)}, f32[1024]{0:T(1024)}, u32[]{:S(2)}) copy-start(f32[1024]{0:T(1024)} %param.24) | copy-start | bytes 12292
  337.7 8.2 copy-start.8
  337.8 8.2 copy-start.9
  428.7 234.1 %reduce-scatter.5.cloned.1.call-start = ((), (), s32[]{:S(2)}) async-start(), calls=%async_computation.3 | async-start | bytes 15728640 | tf_op jit(solution)/shard_map/reduce_scatter | solution.py:148
  428.7 1.0 copy-start.11
  428.7 1.0 copy-start.13
  429.4 422.2 %all-reduce.6.cloned.1.call-start = ((), (), s32[]{:S(2)}) async-start(), calls=%async_computation.5 | async-start | bytes 16777216 | tf_op jit(solution)/shard_map/psum | solution.py:166
  662.8 3.8 copy-start.14
  665.4 1.2 copy-start.3
  672.5 5.3 copy-start.2
  672.5 6.0 copy-start.4
Sparse Core Ops, SparseCore 0:
  12.5 118.0 all-gather.1
  428.8 21.3 reduce-scatter.6
  452.6 210.1 reduce-scatter.4
  670.5 181.1 all-reduce.5
where the time goes:
time: 874 us; the launch traced here: 869 us
  waiting for transfers between devices  466 us (53%)
  blocking collectives  163 us (19%)
  matrix products  106 us (12%)
  local copies, waits for them, and re-layouts  65 us (7%)
  other arithmetic  54.5 us (6%)
  between operations  14.3 us (2%)
    reduce_scatter x1, waiting for transfers between devices, shards(): lax.psum_scatter(source_grad, 'row', scatter_dimension=1, tiled=True)  211 us
    psum x1, waiting for transfers between devices, shards(): lax.psum((proj_local, skip_local, dst_local, src_local, bias_local), ('gr...  124 us
    all_gather x1, waiting for transfers between devices, shards(): gathered = lax.all_gather(hidden, 'row', axis=1, tiled=True)  115 us
    psum x1, blocking collectives, shards(): lax.psum((proj_local, skip_local, dst_local, src_local, bias_local), ('gr...  43.4 us
    psum x1, blocking collectives, shards(): lax.psum(jnp.sum(centered * centered * live_col3, axis=(0, 1)), ('graph',...  41.2 us
    psum x1, blocking collectives, shards(): lax.psum((jnp.sum(grad_out, axis=(0, 1)), jnp.sum(grad_out * normed, axis...  39.5 us
    psum x1, blocking collectives, shards(): real_count, total_sum = lax.psum((count_local, sum_local), ('graph', 'row'))  38.8 us
    sub x3, matrix products, back_core(): grad_shares - spread  37.3 us
  transfers between devices with their start and end apart: 4, of which 4 were waited for; matrix products, arithmetic and copies ran while one was open for 3% of the time, Pallas kernels for 0%

commit v1 on v0

v1 whole, which is shorter than its diff:
```python
import functools

import jax
import jax.numpy as jnp
from jax import lax
from jax.experimental import pallas as pl
from jax.experimental.pallas import tpu as pltpu
from jax.sharding import PartitionSpec as P

EPSILON = 1e-05
MESH = pl.DeviceIdType.MESH
LOG2E = 1.4426950408889634
LN2 = 0.6931471805599453
MASKED = -1e30
TILE = 16
F32 = jnp.float32
BF16 = jnp.bfloat16
ANY = pl.BlockSpec(memory_space=pl.ANY)
VMEM = pl.BlockSpec(memory_space=pltpu.VMEM)
SMEM = pl.BlockSpec(memory_space=pltpu.SMEM)


def dot(left, right, dims=(1, 0)):
    contract = (((dims[0],), (dims[1],)), ((), ()))
    return lax.dot_general(left, right, contract, preferred_element_type=F32)


class Place:
    def __init__(self, planes, slots, group):
        self.planes, self.slots, self.group = planes, slots, group
        self.g = lax.axis_index("graph")
        self.z = lax.axis_index("row")
        self.core = lax.rem(self.g, 2)
        turn = jnp.where(self.core == 1, self.z, planes - 1 - self.z)
        self.mine = [turn == self.turn(s) for s in range(slots)]
        self.slot = sum(jnp.where(own, s, 0) for s, own in enumerate(self.mine))
        self.works = functools.reduce(jnp.logical_or, self.mine)

    def turn(self, slot):
        return slot * self.planes // (self.slots + 1)

    def owner(self, slot):
        turn = self.turn(slot)
        return jnp.where(self.core == 1, turn, self.planes - 1 - turn)


def elu_pair(value):
    grown = jnp.exp(jnp.minimum(value, 0.0))
    return jnp.where(value > 0, value, grown - 1.0), grown


def sub_rows(index, size):
    return pl.ds(pl.multiple_of(index * size, size), size)


def forward_kernel(
    dims,
    feat,
    adj,
    cot,
    counts,
    wp_in,
    ws_in,
    att_rows,
    att_cols,
    bias,
    gain,
    shift,
    feat_out,
    hid_out,
    grad_out,
    norm_out,
    p_out,
    q_out,
    cols_out,
    parts_out,
    sums_out,
    cot_all,
    feat_all,
    hid,
    mask_all,
    mask_own,
    adj_in,
    wp,
    ws,
    pre,
    mix,
    diff,
    low,
    dcol,
    srow,
    p_slot,
    q_slot,
    centered,
    stat,
    stats_a,
    stats_b,
    f_send,
    f_recv,
    a_send,
    a_recv,
    c_send,
    c_recv,
    sa_send,
    sa_recv,
    sb_send,
    sb_recv,
    own_sem,
    adj_sem,
    w_sem,
    p_sem,
    out_sem,
    cot_sem,
):
    planes, group, slots, rows, nodes, heads, head = dims
    width = heads * head
    at = Place(planes, slots, group)
    g, z = at.g, at.z
    block = sub_rows(z, rows)

    barrier = pltpu.get_barrier_semaphore()
    for k in range(1, planes):
        pl.semaphore_signal(barrier, 1, device_id=(g, lax.rem(z + k, planes)), device_id_type=MESH)
    for k in range(1, group):
        pl.semaphore_signal(barrier, 1, device_id=(lax.rem(g + k, group), z), device_id_type=MESH)
    load_wp = pltpu.make_async_copy(wp_in, wp, w_sem.at[0])
    load_ws = pltpu.make_async_copy(ws_in, ws, w_sem.at[1])
    load_wp.start()
    load_ws.start()
    half = rows // 2
    loads = [
        pltpu.make_async_copy(
            adj.at[i // 2, pl.ds(i % 2 * half, half)], adj_in.at[i % 2], adj_sem.at[i % 2]
        )
        for i in range(2 * slots)
    ]
    loads[0].start()
    loads[1].start()
    pl.semaphore_wait(barrier, planes - 1 + group - 1)

    def moves(source, target, send, recv, own):
        out = []
        for s in range(slots):
            to = at.owner(s)
            remote = pltpu.make_async_remote_copy(
                src_ref=source.at[s],
                dst_ref=target.at[block],
                send_sem=send.at[s],
                recv_sem=recv.at[z],
                device_id=(g, to),
                device_id_type=MESH,
            )
            local = pltpu.make_async_copy(source.at[s], target.at[block], own)
            out.append((to, remote, local))
        return out

    def start(copies):
        for to, remote, local in copies:
            pl.when(to != z)(remote.start)
            pl.when(to == z)(local.start)

    def sent(copies):
        for to, remote, local in copies:
            pl.when(to != z)(remote.wait_send)

    def arrived(k, source, target, send, recv, own):
        src = lax.rem(z + k, planes)
        there = target.at[sub_rows(src, rows)]

        @pl.when(k == 0)
        def _():
            pltpu.make_async_copy(source.at[0], there, own).wait()

        @pl.when(k != 0)
        def _():
            pltpu.make_async_remote_copy(
                src_ref=source.at[0],
                dst_ref=there,
                send_sem=send.at[0],
                recv_sem=recv.at[src],
                device_id=(g, src),
                device_id_type=MESH,
            ).wait_recv()

        return src

    f_args = (feat, feat_all, f_send, f_recv, own_sem.at[0])
    a_args = (mask_own, mask_all, a_send, a_recv, own_sem.at[1])
    c_args = (cot, cot_all, c_send, c_recv, own_sem.at[2])
    f_moves, a_moves, c_moves = moves(*f_args), moves(*a_args), moves(*c_args)
    start(f_moves)

    for i, load in enumerate(loads):
        load.wait()
        live_count = counts[i // 2]

        @pl.loop(0, half // TILE)
        def _(t):
            first = i % 2 * half + t * TILE
            shape = (TILE, nodes)
            row = lax.broadcasted_iota(jnp.int32, shape, 0) + (z * rows + first)
            col = lax.broadcasted_iota(jnp.int32, shape, 1)
            allowed = (adj_in[i % 2, sub_rows(t, TILE), :] > 0) | (row == col)
            allowed = allowed & (row < live_count) & (col < live_count)
            mask_own[i // 2, pl.ds(pl.multiple_of(first, TILE), TILE), :] = jnp.where(
                allowed, 0.0, MASKED
            ).astype(BF16)

        if i + 2 < len(loads):
            loads[i + 2].start()

    load_wp.wait()
    load_ws.wait()
    sent(f_moves)
    start(a_moves)
    start(c_moves)

    @pl.when(at.works)
    def _():
        live_count = counts[at.slot]

        @pl.loop(0, planes)
        def _(k):
            src = arrived(k, *f_args)
            here = sub_rows(src, rows)
            value = feat_all[here, :]
            for h in range(heads):
                part = slice(h * head, (h + 1) * head)
                hid[here, part] = dot(value, wp[:, part]).astype(BF16)
                pre[here, part] = dot(value, ws[:, part])
            made = hid[here, :]
            dcol[here, :] = dot(made, att_cols[...]) * LOG2E
            srow[:, here] = dot(att_rows[...], made, (1, 1)) * LOG2E

        pltpu.make_async_copy(feat_all, feat_out, out_sem.at[0]).start()
        pltpu.make_async_copy(hid, hid_out, out_sem.at[1]).start()

        @pl.loop(0, planes)
        def _(k):
            src = arrived(k, *a_args)
            here = sub_rows(src, rows)
            for h in range(heads):
                part = slice(h * head, (h + 1) * head)
                slot = h % 2

                def stores(of):
                    return [
                        pltpu.make_async_copy(kept.at[slot], out.at[h, here], p_sem.at[i, slot])
                        for i, (kept, out) in enumerate(((p_slot, p_out), (q_slot, q_out)))
                    ]

                @pl.when((k > 0) | (h >= 2))
                def _():
                    for store in stores(h):
                        store.wait()

                @pl.loop(0, rows // TILE)
                def _(t):
                    first = src * rows + t * TILE
                    there = pl.ds(pl.multiple_of(first, TILE), TILE)
                    inside = sub_rows(t, TILE)
                    masked = mask_all[there, :].astype(F32) + srow[h : h + 1, :]
                    dst = dcol[there, heads + h : heads + h + 1]
                    node = lax.broadcasted_iota(jnp.int32, (TILE, 1), 0) + first
                    live = (node < live_count).astype(F32)

                    def leaky(raw):
                        small = jnp.exp2(-jnp.abs(raw))
                        soft = jnp.log(1.0 + small)
                        return soft + jnp.maximum(raw * (1.25 * LN2), raw * (0.25 * LN2)), soft

                    peak, _ = leaky(jnp.max(masked, axis=1, keepdims=True) + dst)
                    raw = masked + dst
                    logit, soft = leaky(raw)
                    weight = jnp.exp2((logit - peak) * (0.8 * LOG2E))
                    total = jnp.sum(weight, axis=1, keepdims=True)
                    share = weight * (live / total)
                    slope = jnp.exp2(jnp.minimum(raw, 0.0) - soft * LOG2E) * 0.8 + 0.2
                    sloped = share * slope
                    p_slot[slot, inside, :] = share.astype(BF16)
                    q_slot[slot, inside, :] = sloped.astype(BF16)
                    middle = jnp.sum(sloped, axis=1, keepdims=True)
                    centered[inside, :] = (sloped - middle * share).astype(BF16)

                for store in stores(h):
                    store.start()
                mixed = dot(p_slot[slot], hid[:, part])
                mix[here, part] = mixed
                pre[here, part] += mixed + bias[:, part]
                diff[here, part] = dot(centered[...], hid[:, part]).astype(BF16)

    zero = jnp.zeros((8, width), F32)

    @pl.when(at.works)
    def _():
        live_count = counts[at.slot]

        def live_of(t):
            node = lax.broadcasted_iota(jnp.int32, (TILE, 1), 0) + t * TILE
            return (node < live_count).astype(F32)

        def fold(value):
            return sum(value[8 * i : 8 * i + 8] for i in range(TILE // 8))

        def add_act(t, total):
            act, _ = elu_pair(pre[sub_rows(t, TILE), :])
            return total + fold(act * live_of(t))

        total = lax.fori_loop(0, nodes // TILE, add_act, zero)
        number = jnp.maximum(live_count, 1).astype(F32)
        mean = jnp.sum(total, axis=0, keepdims=True) / number

        def add_square(t, total):
            act, _ = elu_pair(pre[sub_rows(t, TILE), :])
            off = act - mean
            return total + fold(off * off * live_of(t))

        square = lax.fori_loop(0, nodes // TILE, add_square, zero)

        for k in range(planes):
            src = arrived(jnp.int32(k), *c_args)
        pltpu.make_async_copy(feat_all, feat_out, out_sem.at[0]).wait()
        load = pltpu.make_async_copy(cot_all, feat_all, cot_sem)
        load.start()
        load.wait()

        def add_grad(t, totals):
            here = sub_rows(t, TILE)
            act, _ = elu_pair(pre[here, :])
            grad = feat_all[here, :].astype(F32) * live_of(t)
            return totals[0] + fold(grad), totals[1] + fold(grad * (act - mean))

        plain, along = lax.fori_loop(0, nodes // TILE, add_grad, (zero, zero))
        stat[0:1, :] = jnp.full((1, width), live_count.astype(F32))
        stat[1:2, :] = mean
        stat[2:3, :] = jnp.sum(square, axis=0, keepdims=True)
        stat[3:4, :] = jnp.sum(plain, axis=0, keepdims=True)
        stat[4:5, :] = jnp.sum(along, axis=0, keepdims=True)
        stat[5:8, :] = jnp.zeros((3, width), F32)

    @pl.when(jnp.logical_not(at.works))
    def _():
        stat[...] = zero

    def combine(count, one):
        number = sum(one(i, 0) for i in range(count))
        safe = jnp.maximum(number, 1.0)
        mean = sum(one(i, 0) * one(i, 1) for i in range(count)) / safe
        square = sum(
            one(i, 2) + one(i, 0) * (one(i, 1) - mean) * (one(i, 1) - mean) for i in range(count)
        )
        plain = sum(one(i, 3) for i in range(count))
        along = sum(one(i, 4) + one(i, 3) * (one(i, 1) - mean) for i in range(count))
        return number, mean, square, plain, along

    def exchange(size, me, slots_ref, send, recv, device):
        copies = []
        for k in range(1, size):
            peer = lax.rem(me + k, size)
            copy = pltpu.make_async_remote_copy(
                src_ref=stat,
                dst_ref=slots_ref.at[me],
                send_sem=send.at[k],
                recv_sem=recv.at[me],
                device_id=device(peer),
                device_id_type=MESH,
            )
            copy.start()
            copies.append(copy)
        slots_ref[me] = stat[...]
        for k in range(1, size):
            peer = lax.rem(me + k, size)
            pltpu.make_async_remote_copy(
                src_ref=stat,
                dst_ref=slots_ref.at[peer],
                send_sem=send.at[k],
                recv_sem=recv.at[peer],
                device_id=device(peer),
                device_id_type=MESH,
            ).wait_recv()
        for copy in copies:
            copy.wait_send()
        return combine(size, lambda i, j: slots_ref[i, j : j + 1, :])

    sums = exchange(group, g, stats_a, sa_send, sa_recv, lambda peer: (peer, z))
    for j, value in enumerate(sums):
        stat[j : j + 1, :] = value
    number, mean, square, shift_grad, along = exchange(
        planes, z, stats_b, sb_send, sb_recv, lambda peer: (g, peer)
    )
    inv_std = lax.rsqrt(square / number + EPSILON)
    gain_grad = along * inv_std
    sums_out[0:1, :] = gain_grad
    sums_out[1:2, :] = shift_grad
    scale = gain[...] * inv_std
    shift_mean = shift_grad / number
    gain_mean = gain_grad / number

    @pl.when(at.works)
    def _():
        live_count = counts[at.slot]

        def finish(t, total):
            here = sub_rows(t, TILE)
            node = lax.broadcasted_iota(jnp.int32, (TILE, 1), 0) + t * TILE
            live = (node < live_count).astype(F32)
            act, grown = elu_pair(pre[here, :])
            normed = (act - mean) * inv_std
            norm_low = ((gain[...] * normed + shift[...]) * live).astype(BF16)
            cot_value = feat_all[here, :].astype(F32) * live
            feat_all[here, :] = norm_low
            grad = scale * (cot_value - shift_mean - normed * gain_mean) * live
            grad = grad * grown
            grad_low = grad.astype(BF16)
            low[here, :] = grad_low
            grad_low = grad_low.astype(F32)
            lane = lax.broadcasted_iota(jnp.int32, (TILE, 128), 1)
            along_mix = grad_low * mix[here, :]
            along_diff = grad_low * diff[here, :]
            spread = jnp.zeros((TILE, 128), F32)
            for h in range(heads):
                part = slice(h * head, (h + 1) * head)
                one = jnp.sum(along_mix[:, part], axis=1, keepdims=True)
                two = jnp.sum(along_diff[:, part], axis=1, keepdims=True)
                spread = jnp.where(lane % heads == h, one, spread)
                dcol[here, h : h + 1] = two
            top = spread.astype(BF16)
            rest = spread - top.astype(F32)
            middle = rest.astype(BF16)
            bottom = (rest - middle.astype(F32)).astype(BF16)
            third = lane // heads
            mask_all[here, 0:128] = jnp.where(
                third == 0, top, jnp.where(third == 1, middle, jnp.where(third == 2, bottom, 0.0))
            ).astype(BF16)
            return total + sum(grad[8 * i : 8 * i + 8] for i in range(TILE // 8))

        total = lax.fori_loop(0, nodes // TILE, finish, zero)
        sums_out[2:3, :] = jnp.sum(total, axis=0, keepdims=True)
        sums_out[3:8, :] = jnp.zeros((5, width), F32)
        last = [
            pltpu.make_async_copy(low, grad_out, out_sem.at[2]),
            pltpu.make_async_copy(feat_all, norm_out, out_sem.at[3]),
            pltpu.make_async_copy(dcol, cols_out, out_sem.at[4]),
            pltpu.make_async_copy(mask_all.at[:, 0:128], parts_out, out_sem.at[5]),
        ]
        for copy in last:
            copy.start()
        for slot in range(2):
            for i, kept in enumerate((p_slot, q_slot)):
                pltpu.make_async_copy(
                    kept.at[slot], (p_out, q_out)[i].at[0, block], p_sem.at[i, slot]
                ).wait()
        pltpu.make_async_copy(hid, hid_out, out_sem.at[1]).wait()
        for copy in last:
            copy.wait()

    @pl.when(jnp.logical_not(at.works))
    def _():
        sums_out[2:8, :] = jnp.zeros((6, width), F32)

    sent(a_moves)
    sent(c_moves)


def backward_kernel(
    dims,
    feat_in,
    hid_in,
    low_in,
    norm_in,
    p_in,
    q_in,
    cols,
    parts,
    wp_in,
    ws_in,
    att,
    out,
    ig_out,
    proj_out,
    skip_out,
    att_out,
    feat,
    hid,
    low,
    back,
    wp,
    ws,
    ig,
    p_slot,
    q_slot,
    n_send,
    n_recv,
    i_send,
    i_recv,
    own_sem,
    in_sem,
    p_sem,
):
    planes, group, slots, rows, nodes, heads, head = dims
    width = heads * head
    at = Place(planes, slots, group)
    g, z = at.g, at.z
    block = sub_rows(z, rows)

    barrier = pltpu.get_barrier_semaphore()
    for k in range(1, planes):
        pl.semaphore_signal(barrier, 1, device_id=(g, lax.rem(z + k, planes)), device_id_type=MESH)
    loads = [
        pltpu.make_async_copy(source, target, in_sem.at[i])
        for i, (source, target) in enumerate(
            ((feat_in, feat), (hid_in, hid), (low_in, low), (wp_in, wp), (ws_in, ws))
        )
    ]

    def fetch(j, h, slot):
        place = pl.ds(pl.multiple_of(j * rows, rows), rows)
        return [
            pltpu.make_async_copy(kept.at[h, :, place], held.at[slot], p_sem.at[i, slot])
            for i, (kept, held) in enumerate(((p_in, p_slot), (q_in, q_slot)))
        ]

    @pl.when(at.works)
    def _():
        for load in loads:
            load.start()
        for copy in fetch(lax.rem(z + 1, planes), 0, 0):
            copy.start()

    pl.semaphore_wait(barrier, planes - 1)

    def send(source, target, send_sems, recv, to):
        return pltpu.make_async_remote_copy(
            src_ref=source.at[sub_rows(to, rows)],
            dst_ref=target.at[at.slot],
            send_sem=send_sems.at[to],
            recv_sem=recv.at[at.slot],
            device_id=(g, to),
            device_id_type=MESH,
        )

    norm_own = pltpu.make_async_copy(norm_in.at[block], out.at[at.slot], own_sem.at[0])
    ig_own = pltpu.make_async_copy(ig.at[block], ig_out.at[at.slot], own_sem.at[1])

    @pl.when(at.works)
    def _():
        for k in range(1, planes):
            send(norm_in, out, n_send, n_recv, lax.rem(z + k, planes)).start()
        norm_own.start()
        for load in loads:
            load.wait()

        @pl.loop(0, width // head)
        def _(f):
            place = sub_rows(f, head)
            skip_out[place, :] = dot(feat[:, place], low[...], (0, 0)).astype(skip_out.dtype)

        att_out[...] = jnp.zeros_like(att_out)

        @pl.loop(0, planes)
        def _(k):
            j = lax.rem(z + 1 + k, planes)
            here = sub_rows(j, rows)
            for h in range(heads):
                part = slice(h * head, (h + 1) * head)
                slot = h % 2
                if h + 1 < heads:
                    for copy in fetch(j, h + 1, (h + 1) % 2):
                        copy.start()
                else:

                    @pl.when(k + 1 < planes)
                    def _():
                        for copy in fetch(lax.rem(j + 1, planes), 0, heads % 2):
                            copy.start()

                for copy in fetch(j, h, slot):
                    copy.wait()
                grad = dot(p_slot[slot], low[:, part], (0, 0))
                along = dot(q_slot[slot], low[:, part], (0, 0))
                spread = dot(q_slot[slot], parts[...], (0, 0))
                lane = lax.broadcasted_iota(jnp.int32, spread.shape, 1)
                mine = (lane % heads == h) & (lane < 3 * heads)
                own = hid[here, part].astype(F32)
                by_src = jnp.sum(own * along, axis=1, keepdims=True) - jnp.sum(
                    jnp.where(mine, spread, 0.0), axis=1, keepdims=True
                )
                by_dst = cols[here, h : h + 1]
                grad = grad + by_dst * att[h : h + 1, :] + by_src * att[heads + h : heads + h + 1, :]
                back[here, part] = grad.astype(BF16)
                att_out[h : h + 1, :] += jnp.sum(by_dst * own, axis=0, keepdims=True)
                att_out[heads + h : heads + h + 1, :] += jnp.sum(by_src * own, axis=0, keepdims=True)
            for f in range(width // head):
                part = slice(f * head, (f + 1) * head)
                ig[here, part] = (
                    dot(back[here, :], wp[part, :], (1, 1)) + dot(low[here, :], ws[part, :], (1, 1))
                ).astype(BF16)

            @pl.when(j != z)
            def _():
                send(ig, ig_out, i_send, i_recv, j).start()

            pl.when(j == z)(ig_own.start)

        @pl.loop(0, width // head)
        def _(f):
            place = sub_rows(f, head)
            proj_out[place, :] = dot(feat[:, place], back[...], (0, 0)).astype(proj_out.dtype)

    @pl.when(jnp.logical_not(at.works))
    def _():
        proj_out[...] = jnp.zeros_like(proj_out)
        skip_out[...] = jnp.zeros_like(skip_out)
        att_out[...] = jnp.zeros_like(att_out)

    for s in range(slots):
        for source, target, send_sems, recv in (
            (norm_in, out, n_send, n_recv),
            (ig, ig_out, i_send, i_recv),
        ):

            @pl.when(jnp.logical_not(at.mine[s]))
            def _():
                pltpu.make_async_remote_copy(
                    src_ref=source.at[sub_rows(0, rows)],
                    dst_ref=target.at[s],
                    send_sem=send_sems.at[0],
                    recv_sem=recv.at[s],
                    device_id=(g, at.owner(s)),
                    device_id_type=MESH,
                ).wait_recv()

    @pl.when(at.works)
    def _():
        norm_own.wait()
        ig_own.wait()
        for k in range(1, planes):
            to = lax.rem(z + k, planes)
            send(norm_in, out, n_send, n_recv, to).wait_send()
            send(ig, ig_out, i_send, i_recv, to).wait_send()


def params(collective_id):
    return pltpu.CompilerParams(
        collective_id=collective_id, has_side_effects=True, vmem_limit_bytes=60 * 2**20
    )


def shards(
    planes,
    group,
    features,
    adjacency,
    counts,
    proj_weight,
    skip_weight,
    attn_dst,
    attn_src,
    attn_bias,
    norm_gain,
    norm_shift,
    cotangent,
):
    slots, rows, width_in = features.shape
    nodes = adjacency.shape[2]
    heads, head = attn_dst.shape
    width = heads * head
    dims = (planes, group, slots, rows, nodes, heads, head)
    dma = pltpu.SemaphoreType.DMA

    own = jnp.repeat(jnp.eye(heads, dtype=BF16), head, axis=1)
    dst_row, src_row = own * attn_dst.reshape(1, width), own * attn_src.reshape(1, width)
    att_rows = jnp.concatenate([src_row, dst_row, jnp.zeros((16 - 2 * heads, width), BF16)])
    att_cols = jnp.pad(att_rows.T, ((0, 0), (0, 112)))
    att_both = jnp.concatenate([attn_dst, attn_src]).astype(F32)

    shape = jax.ShapeDtypeStruct
    whole = shape((nodes, width), BF16)
    square = shape((heads, nodes, nodes), BF16)
    feat_all, hid, low, norm, p_all, q_all, cols, parts, sums, _ = pl.pallas_call(
        functools.partial(forward_kernel, dims),
        out_shape=[
            shape((nodes, width_in), BF16),
            whole,
            whole,
            whole,
            square,
            square,
            shape((nodes, 128), F32),
            shape((nodes, 128), BF16),
            shape((8, width), F32),
            whole,
        ],
        in_specs=[ANY, ANY, ANY, SMEM, ANY, ANY, VMEM, VMEM, VMEM, VMEM, VMEM],
        out_specs=[ANY] * 8 + [VMEM, ANY],
        scratch_shapes=[
            pltpu.VMEM((nodes, width_in), BF16),
            pltpu.VMEM((nodes, width), BF16),
            pltpu.VMEM((nodes, nodes), BF16),
            pltpu.VMEM((slots, rows, nodes), BF16),
            pltpu.VMEM((2, rows // 2, nodes), jnp.int32),
            pltpu.VMEM((width_in, width), BF16),
            pltpu.VMEM((width_in, width), BF16),
            pltpu.VMEM((nodes, width), F32),
            pltpu.VMEM((nodes, width), F32),
            pltpu.VMEM((nodes, width), BF16),
            pltpu.VMEM((nodes, width), BF16),
            pltpu.VMEM((nodes, 128), F32),
            pltpu.VMEM((16, nodes), F32),
            pltpu.VMEM((2, rows, nodes), BF16),
            pltpu.VMEM((2, rows, nodes), BF16),
            pltpu.VMEM((rows, nodes), BF16),
            pltpu.VMEM((8, width), F32),
            pltpu.VMEM((group, 8, width), F32),
            pltpu.VMEM((planes, 8, width), F32),
            dma((slots,)),
            dma((planes,)),
            dma((slots,)),
            dma((planes,)),
            dma((slots,)),
            dma((planes,)),
            dma((group,)),
            dma((group,)),
            dma((planes,)),
            dma((planes,)),
            dma((3,)),
            dma((2,)),
            dma((2,)),
            dma((2, 2)),
            dma((6,)),
            dma,
        ],
        compiler_params=params(0),
    )(
        features,
        adjacency,
        cotangent,
        counts,
        proj_weight,
        skip_weight,
        att_rows,
        att_cols,
        attn_bias.reshape(1, width),
        norm_gain.reshape(1, width),
        norm_shift.reshape(1, width),
    )
    output, input_grad, proj_local, skip_local, att_local = pl.pallas_call(
        functools.partial(backward_kernel, dims),
        out_shape=[
            shape((slots, rows, width), BF16),
            shape((slots, rows, width_in), BF16),
            shape((width_in, width), BF16),
            shape((width_in, width), BF16),
            shape((2 * heads, head), F32),
        ],
        in_specs=[ANY] * 6 + [VMEM, VMEM, ANY, ANY, VMEM],
        out_specs=[ANY, ANY, VMEM, VMEM, VMEM],
        scratch_shapes=[
            pltpu.VMEM((nodes, width_in), BF16),
            pltpu.VMEM((nodes, width), BF16),
            pltpu.VMEM((nodes, width), BF16),
            pltpu.VMEM((nodes, width), BF16),
            pltpu.VMEM((width_in, width), BF16),
            pltpu.VMEM((width_in, width), BF16),
            pltpu.VMEM((nodes, width_in), BF16),
            pltpu.VMEM((2, nodes, rows), BF16),
            pltpu.VMEM((2, nodes, rows), BF16),
            dma((planes,)),
            dma((slots,)),
            dma((planes,)),
            dma((slots,)),
            dma((2,)),
            dma((5,)),
            dma((2, 2)),
        ],
        compiler_params=params(1),
    )(feat_all, hid, low, norm, p_all, q_all, cols, parts, proj_weight, skip_weight, att_both)
    proj_grad, skip_grad = lax.psum((proj_local, skip_local), ("graph", "row"))
    att_grad, bias_grad = lax.psum((att_local, sums[2]), ("graph", "row"))
    return (
        output,
        input_grad,
        proj_grad.astype(F32),
        skip_grad.astype(F32),
        att_grad[:heads],
        att_grad[heads:],
        bias_grad,
        sums[0],
        sums[1],
    )


def solution(mesh):
    placed = (
        P("graph", "row", None),
        P("graph", "row", None),
        P("graph"),
        P(),
        P(),
        P(),
        P(),
        P(),
        P(),
        P(),
        P("graph", "row", None),
    )
    return jax.shard_map(
        functools.partial(shards, mesh.shape["row"], mesh.shape["graph"]),
        mesh=mesh,
        in_specs=placed,
        out_specs=(
            P("graph", "row", None),
            P("graph", "row", None),
            P(),
            P(),
            P(),
            P(),
            P(),
            P(),
            P(),
        ),
        check_vma=False,
    )
```

time: 874 us -> 443 us (0.51)
  waiting for transfers between devices: 466 us -> 99.7 us
  Pallas kernels: 0 us -> 264 us
  blocking collectives: 163 us -> 48.9 us
  matrix products: 106 us -> 0 us
  local copies, waits for them, and re-layouts: 65 us -> 7.67 us
  other arithmetic: 54.5 us -> 8.1 us
    pallas_call x0 -> x2, Pallas kernels: none -> 264 us  [the longest x1 188 us: shards(): pl.pallas_call(functools.partial(forward_kernel, dims), out_shape=[shape(...]
    reduce_scatter x1 -> x0, waiting for transfers between devices: 211 us -> none  [shards(): lax.psum_scatter(source_grad, 'row', scatter_dimension=1, tiled=True)]
    all_gather x1 -> x0, waiting for transfers between devices: 115 us -> none  [shards(): gathered = lax.all_gather(hidden, 'row', axis=1, tiled=True)]
    psum x4 -> x1, blocking collectives: 163 us -> 48.9 us  [shards(): att_grad, bias_grad = lax.psum((att_local, sums[2]), ('graph', 'row'))]
    dot_general x16 -> x0, matrix products: 68.4 us -> none  [the longest x3 16.2 us: attend(): jnp.einsum('hrn,nhc->rhc', shares, source.reshape(node_total, head_count,...]
    sub x3 -> x0, matrix products: 37.3 us -> none  [back_core(): grad_shares - spread]
    reduce_sum x8 -> x0, other arithmetic: 29.4 us -> none  [the longest x3 11.7 us: attend(): totals = jnp.sum(weight, axis=2) + (1.0 - live_row)[None, :]]
    unnamed x41 -> x16, local copies, waits for them, and re-layouts: 29.9 us -> 4.58 us
  transfers between devices with their start and end apart: 4 -> 1, of which waited for: 4 -> 1; matrix products, arithmetic and copies ran while one was open for 3% -> 0% of each run, Pallas kernels for 0% -> 0%
where the time goes in v1:
time: 443 us
  Pallas kernels  264 us (60%)
  waiting for transfers between devices  99.7 us (23%)
  blocking collectives  48.9 us (11%)
  between operations  14.1 us (3%)
  other arithmetic  8.1 us (2%)
  local copies, waits for them, and re-layouts  7.67 us (2%)
    pallas_call x1, Pallas kernels, shards(): pl.pallas_call(functools.partial(forward_kernel, dims), out_shape=[shape(...  188 us
    psum x1, waiting for transfers between devices, shards(): proj_grad, skip_grad = lax.psum((proj_local, skip_local), ('graph', 'row'))  99.6 us
    pallas_call x1, Pallas kernels, shards(): pl.pallas_call(functools.partial(backward_kernel, dims), out_shape=[shape...  76.5 us
    psum x1, blocking collectives, shards(): att_grad, bias_grad = lax.psum((att_local, sums[2]), ('graph', 'row'))  48.9 us
  transfers between devices with their start and end apart: 1, of which 1 were waited for; matrix products, arithmetic and copies ran while one was open for 0% of the time, Pallas kernels for 0%

profile of v1, /device:TPU:0, one launch (start us, length us, event | category | flops | bytes accessed | tf_op | source)
XLA Modules:
  0.0 442.8 jit_solution(14862675299264699482)
XLA Ops:
  7.2 0.0 all-reduce.5.cloned.1.call-start
  7.2 0.7 copy.23
  7.9 1.3 maximum_convert_fusion.att
  9.2 0.7 copy.24
  9.9 0.1 broadcast_bitcast_fusion
  10.0 0.1 pad.9.clone
  10.1 0.1 maximum_maximum_fusion.att_rows
  10.2 0.2 copy.21
  10.3 0.8 pad.4.att_cols
  11.1 0.0 copy-done.3
  11.1 187.9 %shard_map.178 = (bf16[1024,1024]{1,0:T(8,128)(2,1)}, bf16[1024,1024]{1,0:T(8,128)(2,1)}, bf16[1024,1024]{1,0:T(8,128)(2,1)}, bf16[1024,1024]{1,0:T(8,128)(2,1)}...) custom-call(bf16[3,256,1024]{2,1,0:T(8,128)(2,1)} %feat.1, ...), custom_call_target="tpu_custom_call" | custom-call | tf_op jit(solution)/shard_map/pallas_call | solution.py:680
  199.0 76.5 %shard_map.179 = (bf16[3,256,1024]{2,1,0:T(8,128)(2,1)}, bf16[3,256,1024]{2,1,0:T(8,128)(2,1)}, bf16[1024,1024]{1,0:T(8,128)(2,1)}, bf16[1024,1024]{1,0:T(8,128)(2,1)}, f32[8,256]{1,0:T(8,128)}) custom-call(bf16[1024,1024]{1,0:T(8,128)(2,1)} %get-tuple-element.23.feat_in, bf16[1024,1024]{1,0:T(8,128)(2,1)} %get-tuple-element.24.hid_in, ...), custom_call_target="tpu_custom_call" | custom-call | tf_op jit(solution)/shard_map/pallas_call | solution.py:747
  275.5 0.0 copy-start.4
  275.5 0.0 all-reduce.5.cloned.1.call-update
  275.5 1.5 fusion.1
  277.0 0.0 copy-done.4
  277.0 48.9 %all-reduce.1 = (f32[8,256]{1,0:T(8,128)S(1)}, f32[1024]{0:T(1024)}) all-reduce(f32[8,256]{1,0:T(8,128)S(1)} %copy-done.4, f32[1024]{0:T(1024)S(1)} %bitcast.16), channel_id=1, replica_groups=mesh['graph'=8,'row'=4] {'graph','row'}, use_global_device_ids=true, to_apply=%region_2.3 | all-reduce | flops 3072 | bytes 24576 | tf_op jit(solution)/shard_map/psum | solution.py:779
  325.9 0.6 fusion.2
  326.5 99.6 %all-reduce.5.cloned.1.call-done = (bf16[1024,1024]{1,0:T(8,128)(2,1)}, bf16[1024,1024]{1,0:T(8,128)(2,1)}) async-done(((bf16[1024,1024]{1,0:T(8,128)(2,1)}, bf16[1024,1024]{1,0:T(8,128)(2,1)}), (bf16[1024,1024]{1,0:T(8,128)(2,1)}, bf16[1024,1024]{1,0:T(8,128)(2,1)})) %all-reduce.5.cloned.1.call-update) | async-done | bytes 4194320 | tf_op jit(solution)/shard_map/psum | solution.py:778
  426.2 4.2 convert_element_type.18
  430.4 2.5 convert_element_type.19
  432.9 1.1 copy.29
  434.0 0.8 copy-done.1
  434.9 1.1 copy.30
  (10 shorter events, 0.0 us)
Async XLA Ops:
  7.2 419.0 %all-reduce.5.cloned.1.call-start = ((), (), s32[]{:S(2)}) async-start(), calls=%async_computation | async-start | bytes 8388608 | tf_op jit(solution)/shard_map/psum | solution.py:778
  10.2 0.9 copy-start.3
  275.5 1.5 copy-start.4
  426.2 4.2 copy-start
  430.4 2.5 copy-start.2
  432.9 2.0 copy-start.1
Sparse Core Ops, SparseCore 0:
  275.7 150.4 all-reduce.4

commit v2 on v0

v2 whole, which is shorter than its diff:
```python
import functools

import jax
import jax.numpy as jnp
from jax import lax
from jax.experimental import pallas as pl
from jax.experimental.pallas import tpu as pltpu
from jax.sharding import PartitionSpec as P

EPSILON = 1e-05
MESH = pl.DeviceIdType.MESH
LOG2E = 1.4426950408889634
LN2 = 0.6931471805599453
MASKED = -1e30
TILE = 64
WIDE_TILE = 256
F32 = jnp.float32
BF16 = jnp.bfloat16
ANY = pl.BlockSpec(memory_space=pl.ANY)
VMEM = pl.BlockSpec(memory_space=pltpu.VMEM)
SMEM = pl.BlockSpec(memory_space=pltpu.SMEM)


def dot(left, right, dims=(1, 0)):
    contract = (((dims[0],), (dims[1],)), ((), ()))
    return lax.dot_general(left, right, contract, preferred_element_type=F32)


class Place:
    def __init__(self, planes, slots, group):
        self.planes, self.slots, self.group = planes, slots, group
        self.g = lax.axis_index("graph")
        self.z = lax.axis_index("row")
        self.core = lax.rem(self.g, 2)
        turn = jnp.where(self.core == 1, self.z, planes - 1 - self.z)
        self.mine = [turn == self.turn(s) for s in range(slots)]
        self.slot = sum(jnp.where(own, s, 0) for s, own in enumerate(self.mine))
        self.works = functools.reduce(jnp.logical_or, self.mine)

    def turn(self, slot):
        return slot * self.planes // (self.slots + 1)

    def owner(self, slot):
        turn = self.turn(slot)
        return jnp.where(self.core == 1, turn, self.planes - 1 - turn)


def elu_pair(value):
    grown = jnp.exp(jnp.minimum(value, 0.0))
    return jnp.where(value > 0, value, grown - 1.0), grown


def sub_rows(index, size):
    return pl.ds(pl.multiple_of(index * size, size), size)


def layer_kernel(
    dims,
    feat,
    adj,
    cot,
    counts,
    wp_in,
    ws_in,
    att_rows,
    att_cols,
    bias,
    gain,
    shift,
    out,
    ig_out,
    proj_out,
    skip_out,
    sums_out,
    p_all,
    q_all,
    feat_all,
    hid,
    wide,
    mask_own,
    adj_in,
    wp,
    ws,
    pre,
    mix,
    diff,
    low,
    dcol,
    parts,
    srow,
    p_slot,
    q_slot,
    centered,
    p_back,
    q_back,
    stat,
    stats_a,
    stats_b,
    swap,
    plane_in,
    line_in,
    line_out,
    f_send,
    f_recv,
    a_send,
    a_recv,
    c_send,
    c_recv,
    n_send,
    n_recv,
    i_send,
    i_recv,
    sa_send,
    sa_recv,
    sb_send,
    sb_recv,
    r_send,
    r_recv,
    own_sem,
    adj_sem,
    w_sem,
    p_sem,
    out_sem,
):
    planes, group, slots, rows, nodes, heads, head, width_in = dims
    width = heads * head
    tile = min(TILE, TILE * 1024 // nodes)
    tall = min(WIDE_TILE * 1024 // nodes * 1024 // nodes, rows)
    at = Place(planes, slots, group)
    g, z = at.g, at.z
    block = sub_rows(z, rows)
    mask_all = wide.at[:, 0:nodes]
    back = wide.at[:, 0:width]
    stage = wide.at[:, width : 2 * width]

    barrier = pltpu.get_barrier_semaphore()
    for k in range(1, planes):
        pl.semaphore_signal(barrier, 1, device_id=(g, lax.rem(z + k, planes)), device_id_type=MESH)
    for k in range(1, group):
        pl.semaphore_signal(barrier, 1, device_id=(lax.rem(g + k, group), z), device_id_type=MESH)
    load_wp = pltpu.make_async_copy(wp_in, wp, w_sem.at[0])
    load_ws = pltpu.make_async_copy(ws_in, ws, w_sem.at[1])
    some = adj_in.shape[1]
    cuts = rows // some
    loads = [
        pltpu.make_async_copy(
            adj.at[i // cuts, pl.ds(i % cuts * some, some)], adj_in.at[i % 2], adj_sem.at[i % 2]
        )
        for i in range(cuts * slots)
    ]
    loads[0].start()
    loads[1].start()
    load_wp.start()
    load_ws.start()
    pl.semaphore_wait(barrier, planes - 1 + group - 1)

    def remote(source, target, send, recv, device):
        return pltpu.make_async_remote_copy(
            src_ref=source,
            dst_ref=target,
            send_sem=send,
            recv_sem=recv,
            device_id=device,
            device_id_type=MESH,
        )

    def moves(source, target, send, recv, own):
        found = []
        for s in range(slots):
            to = at.owner(s)
            away = remote(source.at[s], target.at[block], send.at[s], recv.at[z], (g, to))
            local = pltpu.make_async_copy(source.at[s], target.at[block], own)
            found.append((to, away, local))
        return found

    def start(copies):
        for far in range(1, planes):
            for to, away, _ in copies:
                pl.when(jnp.abs(to - z) == far)(away.start)
        for to, _, local in copies:
            pl.when(to == z)(local.start)

    def sent(copies):
        for to, away, _ in copies:
            pl.when(to != z)(away.wait_send)

    def arrived(k, source, target, send, recv, own):
        src = lax.rem(z + k, planes)
        there = target.at[sub_rows(src, rows)]
        pl.when(k == 0)(pltpu.make_async_copy(source.at[0], there, own).wait)
        pl.when(k != 0)(remote(source.at[0], there, send.at[0], recv.at[src], (g, src)).wait_recv)
        return src

    f_args = (feat, feat_all, f_send, f_recv, own_sem.at[0])
    a_args = (mask_own, mask_all, a_send, a_recv, own_sem.at[1])
    c_args = (cot, low, c_send, c_recv, own_sem.at[2])
    f_moves, a_moves, c_moves = moves(*f_args), moves(*a_args), moves(*c_args)
    start(f_moves)

    for i, load in enumerate(loads):
        load.wait()
        live_own = counts[i // cuts]

        @pl.loop(0, some // tile)
        def _(t):
            first = i % cuts * some + t * tile
            shape = (tile, nodes)
            row = lax.broadcasted_iota(jnp.int32, shape, 0) + (z * rows + first)
            col = lax.broadcasted_iota(jnp.int32, shape, 1)
            allowed = (adj_in[i % 2, sub_rows(t, tile), :] > 0) | (row == col)
            allowed = allowed & (row < live_own) & (col < live_own)
            mask_own[i // cuts, pl.ds(pl.multiple_of(first, tile), tile), :] = jnp.where(
                allowed, 0.0, MASKED
            ).astype(BF16)

        if i + 2 < len(loads):
            loads[i + 2].start()

    load_wp.wait()
    load_ws.wait()
    start(a_moves)
    start(c_moves)
    live_count = counts[at.slot]

    def live_of(first, size):
        node = lax.broadcasted_iota(jnp.int32, (size, 1), 0) + first
        return (node < live_count).astype(F32)

    depth = p_slot.shape[0]

    def keep(h, here):
        slot = h % depth
        return [
            pltpu.make_async_copy(p_slot.at[slot], p_all.at[h, here], p_sem.at[0, slot]),
            pltpu.make_async_copy(q_slot.at[slot], q_all.at[h, here], p_sem.at[1, slot]),
        ]

    @pl.when(at.works)
    def _():
        @pl.loop(0, planes)
        def _(k):
            src = arrived(k, *f_args)
            here = sub_rows(src, rows)
            value = feat_all[here, :]
            for h in range(heads):
                part = slice(h * head, (h + 1) * head)
                hid[here, part] = dot(value, wp[:, part]).astype(BF16)
                pre[here, part] = dot(value, ws[:, part])
            made = hid[here, :]
            dcol[here, :] = dot(made, att_cols[...]) * LOG2E
            srow[:, here] = dot(att_rows[...], made, (1, 1)) * LOG2E

        @pl.loop(0, planes)
        def _(k):
            src = arrived(k, *a_args)
            here = sub_rows(src, rows)
            for h in range(heads):
                part = slice(h * head, (h + 1) * head)
                slot = h % depth

                @pl.when((k > 0) | (h >= depth))
                def _():
                    for copy in keep(h, here):
                        copy.wait()

                @pl.loop(0, rows // tall)
                def _(t):
                    first = src * rows + t * tall
                    there = pl.ds(pl.multiple_of(first, tall), tall)
                    inside = sub_rows(t, tall)
                    masked = mask_all[there, :].astype(F32) + srow[h : h + 1, :]
                    dst = dcol[there, heads + h : heads + h + 1]

                    def leaky(raw):
                        small = jnp.exp2(-jnp.abs(raw))
                        soft = jnp.log(1.0 + small)
                        return soft + jnp.maximum(raw * (1.25 * LN2), raw * (0.25 * LN2)), soft

                    peak, _ = leaky(jnp.max(masked, axis=1, keepdims=True) + dst)
                    raw = masked + dst
                    logit, soft = leaky(raw)
                    weight = jnp.exp2((logit - peak) * (0.8 * LOG2E))
                    total = jnp.sum(weight, axis=1, keepdims=True)
                    share = weight * (live_of(first, tall) / total)
                    slope = jnp.exp2(jnp.minimum(raw, 0.0) - soft * LOG2E) * 0.8 + 0.2
                    sloped = share * slope
                    p_slot[slot, inside, :] = share.astype(BF16)
                    q_slot[slot, inside, :] = sloped.astype(BF16)
                    middle = jnp.sum(sloped, axis=1, keepdims=True)
                    centered[inside, :] = (sloped - middle * share).astype(BF16)

                for copy in keep(h, here):
                    copy.start()
                mixed = dot(p_slot[slot], hid[:, part])
                mix[here, part] = mixed.astype(BF16)
                pre[here, part] += mixed + bias[:, part]
                diff[here, part] = dot(centered[...], hid[:, part]).astype(BF16)

    zero = jnp.zeros((8, width), F32)
    tiles = nodes // tile

    def fold(value):
        return sum(value[8 * i : 8 * i + 8] for i in range(tile // 8))

    def total_of(value):
        return jnp.sum(value, axis=0, keepdims=True)

    @pl.when(at.works)
    def _():
        def add_act(t, total):
            act, _ = elu_pair(pre[sub_rows(t, tile), :])
            return total + fold(act * live_of(t * tile, tile))

        number = jnp.maximum(live_count, 1).astype(F32)
        mean = total_of(lax.fori_loop(0, tiles, add_act, zero)) / number

        def add_square(t, total):
            act, _ = elu_pair(pre[sub_rows(t, tile), :])
            off = act - mean
            return total + fold(off * off * live_of(t * tile, tile))

        stat[2:3, :] = total_of(lax.fori_loop(0, tiles, add_square, zero))
        stat[0:1, :] = jnp.full((1, width), live_count.astype(F32))
        stat[1:2, :] = mean
        stat[3:8, :] = jnp.zeros((5, width), F32)

    @pl.when(jnp.logical_not(at.works))
    def _():
        stat[...] = zero

    def exchange(which, size, me, held, send, recv, device):
        copies = []
        for k in range(1, size):
            peer = lax.rem(me + k, size)
            copy = remote(
                stat, held.at[which, me], send.at[which, k], recv.at[which, me], device(peer)
            )
            copy.start()
            copies.append(copy)
        held[which, me] = stat[...]
        for k in range(1, size):
            peer = lax.rem(me + k, size)
            remote(
                stat, held.at[which, peer], send.at[which, k], recv.at[which, peer], device(peer)
            ).wait_recv()
        for copy in copies:
            copy.wait_send()

    def everywhere(which, combine):
        exchange(which, group, g, stats_a, sa_send, sa_recv, lambda peer: (peer, z))
        combine(stats_a.at[which], group)
        exchange(which, planes, z, stats_b, sb_send, sb_recv, lambda peer: (g, peer))
        combine(stats_b.at[which], planes)

    def spread_out(held, size):
        number = sum(held[i, 0:1, :] for i in range(size))
        mean = sum(held[i, 0:1, :] * held[i, 1:2, :] for i in range(size))
        mean = mean / jnp.maximum(number, 1.0)
        square = zero[0:1]
        for i in range(size):
            off = held[i, 1:2, :] - mean
            square = square + held[i, 2:3, :] + held[i, 0:1, :] * off * off
        stat[0:1, :] = number
        stat[1:2, :] = mean
        stat[2:3, :] = square

    def plain_sum(held, size):
        stat[...] = sum(held[i] for i in range(size))

    everywhere(0, spread_out)
    number, mean = stat[0:1, :], stat[1:2, :]
    inv_std = lax.rsqrt(stat[2:3, :] / number + EPSILON)

    def give(target, send, recv, to):
        return remote(
            stage.at[sub_rows(to, rows)],
            target.at[at.slot],
            send.at[to],
            recv.at[at.slot],
            (g, to),
        )

    norm_own = pltpu.make_async_copy(stage.at[block], out.at[at.slot], own_sem.at[3])
    ig_own = pltpu.make_async_copy(stage.at[block], ig_out.at[at.slot], own_sem.at[4])

    @pl.when(at.works)
    def _():
        @pl.loop(0, planes)
        def _(k):
            j = lax.rem(z + 1 + k, planes)

            @pl.loop(0, rows // tile)
            def _(t):
                first = j * rows + t * tile
                here = pl.ds(pl.multiple_of(first, tile), tile)
                act, _ = elu_pair(pre[here, :])
                normed = (act - mean) * inv_std
                value = (gain[...] * normed + shift[...]) * live_of(first, tile)
                stage[here, :] = value.astype(BF16)

            pl.when(j != z)(give(out, n_send, n_recv, j).start)
            pl.when(j == z)(norm_own.start)

        for k in range(planes):
            arrived(jnp.int32(k), *c_args)

        def add_grad(t, totals):
            here = sub_rows(t, tile)
            act, _ = elu_pair(pre[here, :])
            grad = low[here, :].astype(F32) * live_of(t * tile, tile)
            return totals[0] + fold(grad), totals[1] + fold(grad * (act - mean))

        plain, along = lax.fori_loop(0, tiles, add_grad, (zero, zero))
        stat[0:1, :] = total_of(plain)
        stat[1:2, :] = total_of(along)
        stat[2:8, :] = jnp.zeros((6, width), F32)

    @pl.when(jnp.logical_not(at.works))
    def _():
        stat[...] = zero

    everywhere(1, plain_sum)
    shift_grad = stat[0:1, :]
    gain_grad = stat[1:2, :] * inv_std
    sums_out[0:1, :] = gain_grad
    sums_out[1:2, :] = shift_grad
    scale = gain[...] * inv_std
    shift_mean = shift_grad / number
    gain_mean = gain_grad / number
    stat[...] = zero

    @pl.when(at.works)
    def _():
        def finish(t, total):
            here = sub_rows(t, tile)
            live = live_of(t * tile, tile)
            act, grown = elu_pair(pre[here, :])
            normed = (act - mean) * inv_std
            grad = low[here, :].astype(F32) * live
            grad = scale * (grad - shift_mean - normed * gain_mean) * live * grown
            grad_low = grad.astype(BF16)
            low[here, :] = grad_low
            grad_low = grad_low.astype(F32)
            lane = lax.broadcasted_iota(jnp.int32, (tile, 128), 1)
            along_mix = grad_low * mix[here, :].astype(F32)
            along_diff = grad_low * diff[here, :].astype(F32)
            spread = jnp.zeros((tile, 128), F32)
            for h in range(heads):
                part = slice(h * head, (h + 1) * head)
                one = jnp.sum(along_mix[:, part], axis=1, keepdims=True)
                spread = jnp.where(lane % heads == h, one, spread)
                dcol[here, h : h + 1] = jnp.sum(along_diff[:, part], axis=1, keepdims=True)
            top = spread.astype(BF16)
            rest = spread - top.astype(F32)
            middle = rest.astype(BF16)
            bottom = (rest - middle.astype(F32)).astype(BF16)
            third = lane // heads
            parts[here, :] = jnp.where(
                third == 0, top, jnp.where(third == 1, middle, jnp.where(third == 2, bottom, 0.0))
            ).astype(BF16)
            return total + fold(grad)

        stat[0:1, :] = total_of(lax.fori_loop(0, tiles, finish, zero))
        for h in range(depth):
            for copy in keep(h, block):
                copy.wait()

    chips = group // 2
    chip, core = g // 2, lax.rem(g, 2)
    partner = g + 1 - 2 * core
    half_width = width // 2
    quarter = half_width // 2
    strip = width_in // chips
    down = min(planes, strip // 16)
    across = planes // down
    mine = pl.ds(pl.multiple_of(core * quarter, quarter), quarter)
    other = pl.ds(pl.multiple_of((1 - core) * quarter, quarter), quarter)

    def unit_of(u):
        kept = diff if u < 2 else mix
        return kept.at[0:width_in, u % 2 * half_width : (u % 2 + 1) * half_width]

    def strip_of(index):
        return pl.ds(pl.multiple_of(index * strip, strip), strip)

    def piece_of(index):
        high, wide_piece = strip // down, quarter // across
        return (
            pl.ds(pl.multiple_of(lax.rem(index, down) * high, high), high),
            pl.ds(pl.multiple_of(index // down * wide_piece, wide_piece), wide_piece),
        )

    def to_core(u):
        return remote(
            unit_of(u).at[:, other], swap.at[u], r_send.at[u, 0, 0], r_recv.at[u, 0, 0], (partner, z)
        )

    def to_chip(u, peer, landed):
        return remote(
            unit_of(u).at[strip_of(peer), mine],
            plane_in.at[u, landed],
            r_send.at[u, 1, peer],
            r_recv.at[u, 1, landed],
            (2 * peer + core, z),
        )

    def to_line(u, peer, landed):
        return remote(
            line_out.at[u].at[piece_of(peer)],
            line_in.at[u, landed],
            r_send.at[u, 2, peer],
            r_recv.at[u, 2, landed],
            (g, peer),
        )

    def from_line(u, peer, landed):
        where = swap.at[u].at[strip_of(chip)].at[piece_of(landed)]
        return remote(where, where, r_send.at[u, 3, peer], r_recv.at[u, 3, landed], (g, peer))

    def from_chip(u, peer, landed):
        where = swap.at[u].at[strip_of(landed)]
        return remote(
            where, where, r_send.at[u, 4, peer], r_recv.at[u, 4, landed], (2 * peer + core, z)
        )

    def from_core(u, columns):
        return remote(
            swap.at[u],
            unit_of(u).at[:, columns],
            r_send.at[u, 5, 0],
            r_recv.at[u, 5, 0],
            (partner, z),
        )

    def others(size, me):
        return [lax.rem(me + k, size) for k in range(1, size)]

    def step(u, number):
        unit = unit_of(u)
        if number == 0:
            to_core(u).start()
        if number == 1:
            to_core(u).wait()

            @pl.loop(0, width_in // tall)
            def _(t):
                here = sub_rows(t, tall)
                value = unit[here, mine].astype(F32) + swap[u, here, :].astype(F32)
                unit[here, mine] = value.astype(BF16)

            for peer in others(chips, chip):
                to_chip(u, peer, chip).start()
        if number == 2:
            for peer in others(chips, chip):
                to_chip(u, peer, peer).wait_recv()
            value = unit[strip_of(chip), mine].astype(F32)
            for peer in others(chips, chip):
                value = value + plane_in[u, peer].astype(F32)
            line_out[u] = value.astype(BF16)
            for peer in others(planes, z):
                to_line(u, peer, z).start()
            for peer in others(chips, chip):
                to_chip(u, peer, chip).wait_send()
        if number == 3:
            for peer in others(planes, z):
                to_line(u, peer, peer).wait_recv()
            value = line_out.at[u][piece_of(z)].astype(F32)
            for peer in others(planes, z):
                value = value + line_in[u, peer].astype(F32)
            swap.at[u].at[strip_of(chip)][piece_of(z)] = value.astype(BF16)
            for peer in others(planes, z):
                from_line(u, peer, z).start()
            for peer in others(planes, z):
                to_line(u, peer, z).wait_send()
        if number == 4:
            for peer in others(planes, z):
                from_line(u, peer, peer).wait_recv()
            for peer in others(chips, chip):
                from_chip(u, peer, chip).start()
            for peer in others(planes, z):
                from_line(u, peer, z).wait_send()
        if number == 5:
            for peer in others(chips, chip):
                from_chip(u, peer, peer).wait_recv()
            from_core(u, mine).start()

            @pl.loop(0, width_in // tall)
            def _(t):
                here = sub_rows(t, tall)
                unit[here, mine] = swap[u, here, :]

            for peer in others(chips, chip):
                from_chip(u, peer, chip).wait_send()
        if number == 6:
            from_core(u, other).wait_recv()
            from_core(u, mine).wait_send()
            answer(u).start()

    def answer(u):
        target = skip_out if u < 2 else proj_out
        columns = slice(u % 2 * half_width, (u % 2 + 1) * half_width)
        return pltpu.make_async_copy(unit_of(u), target.at[:, columns], out_sem.at[u])

    def fetch(j, h):
        place = pl.ds(pl.multiple_of(j * rows, rows), rows)
        slot = h % 2
        return [
            pltpu.make_async_copy(p_all.at[h, :, place], p_back.at[slot], p_sem.at[2, slot]),
            pltpu.make_async_copy(q_all.at[h, :, place], q_back.at[slot], p_sem.at[3, slot]),
        ]

    def product(u, right):
        unit = unit_of(u)
        columns = slice(u % 2 * half_width, (u % 2 + 1) * half_width)

        @pl.when(at.works)
        def _():
            @pl.loop(0, width_in // head)
            def _(f):
                place = sub_rows(f, head)
                unit[place, :] = dot(feat_all[:, place], right[:, columns], (0, 0)).astype(BF16)

        @pl.when(jnp.logical_not(at.works))
        def _():
            unit[...] = jnp.zeros_like(unit)

    @pl.when(at.works)
    def _():
        for copy in fetch(lax.rem(z + 1, planes), 0):
            copy.start()

    for u in (0, 1):
        product(u, low)
        step(u, 0)

    def source_block(k, turn):
        j = lax.rem(z + 1 + k, planes)
        here = sub_rows(j, rows)
        per_turn = heads // 2
        for h in range(turn * per_turn, (turn + 1) * per_turn):
            part = slice(h * head, (h + 1) * head)
            slot = h % 2
            if h + 1 < (turn + 1) * per_turn:
                for copy in fetch(j, h + 1):
                    copy.start()
            else:

                @pl.when(k + 1 < planes)
                def _():
                    for copy in fetch(lax.rem(j + 1, planes), turn * per_turn):
                        copy.start()

                if turn == 0:

                    @pl.when(k + 1 == planes)
                    def _():
                        for copy in fetch(lax.rem(z + 1, planes), per_turn):
                            copy.start()

            for copy in fetch(j, h):
                copy.wait()
            grad = dot(p_back[slot], low[:, part], (0, 0))
            along = dot(q_back[slot], low[:, part], (0, 0))
            spread = dot(q_back[slot], parts[...], (0, 0))
            lane = lax.broadcasted_iota(jnp.int32, spread.shape, 1)
            chosen = (lane % heads == h) & (lane < 3 * heads)
            own = hid[here, part].astype(F32)
            by_src = jnp.sum(own * along, axis=1, keepdims=True) - jnp.sum(
                jnp.where(chosen, spread, 0.0), axis=1, keepdims=True
            )
            by_dst = dcol[here, h : h + 1]
            att_src, att_dst = (
                att_rows[i : i + 1, part].astype(F32) for i in (h, heads + h)
            )
            grad = grad + by_dst * att_dst + by_src * att_src
            back[here, part] = grad.astype(BF16)
            stat[1:2, part] += total_of(by_dst * own)
            stat[2:3, part] += total_of(by_src * own)
        if turn == 1:
            pl.when(j != z)(give(out, n_send, n_recv, j).wait_send)
            pl.when(j == z)(norm_own.wait)
            for f in range(width_in // head):
                part = slice(f * head, (f + 1) * head)
                stage[here, part] = (
                    dot(back[here, :], wp[part, :], (1, 1)) + dot(low[here, :], ws[part, :], (1, 1))
                ).astype(BF16)
            pl.when(j != z)(give(ig_out, i_send, i_recv, j).start)
            pl.when(j == z)(ig_own.start)

    for turn in range(2):

        @pl.loop(0, planes)
        def _(k):
            pl.when(at.works)(functools.partial(source_block, k, turn))
            for when, work in PLAN[turn]:

                @pl.when(k == when)
                def _():
                    for u, number in work:
                        step(u, number)

        product(2 + turn, back)
        step(2 + turn, 0)

    for u, number in PLAN[2]:
        step(u, number)
    everywhere(0, plain_sum)
    sums_out[2:5, :] = stat[0:3, :]
    sums_out[5:8, :] = jnp.zeros((3, width), F32)
    for u, number in PLAN[3]:
        step(u, number)

    for s in range(slots):
        for target, send, recv in ((out, n_send, n_recv), (ig_out, i_send, i_recv)):
            pl.when(jnp.logical_not(at.mine[s]))(
                remote(
                    stage.at[sub_rows(0, rows)],
                    target.at[s],
                    send.at[0],
                    recv.at[s],
                    (g, at.owner(s)),
                ).wait_recv
            )

    @pl.when(at.works)
    def _():
        ig_own.wait()
        for peer in others(planes, z):
            give(ig_out, i_send, i_recv, peer).wait_send()

    for u in range(4):
        answer(u).wait()
    sent(f_moves)
    sent(a_moves)
    sent(c_moves)


PLAN = (
    ((0, ((0, 1),)), (1, ((1, 1),)), (3, ((0, 2), (1, 2)))),
    ((0, ((2, 1),)), (1, ((0, 3), (1, 3))), (2, ((2, 2),)), (3, ((0, 4), (1, 4)))),
    ((3, 1), (2, 3), (0, 5), (1, 5), (3, 2), (2, 4), (3, 3), (0, 6), (1, 6)),
    ((2, 5), (3, 4), (2, 6), (3, 5), (3, 6)),
)


def shards(
    planes,
    group,
    features,
    adjacency,
    counts,
    proj_weight,
    skip_weight,
    attn_dst,
    attn_src,
    attn_bias,
    norm_gain,
    norm_shift,
    cotangent,
):
    slots, rows, width_in = features.shape
    nodes = adjacency.shape[2]
    heads, head = attn_dst.shape
    width = heads * head
    dims = (planes, group, slots, rows, nodes, heads, head, width_in)
    dma = pltpu.SemaphoreType.DMA
    chips = group // 2
    strip, quarter = width_in // chips, width // 4
    down = min(planes, strip // 16)
    piece = (strip // down, quarter // (planes // down))
    tallest = max(nodes, width_in)
    depth = 2 if nodes <= 1024 else 1

    own = jnp.repeat(jnp.eye(heads, dtype=BF16), head, axis=1)
    dst_row, src_row = own * attn_dst.reshape(1, width), own * attn_src.reshape(1, width)
    att_rows = jnp.concatenate([src_row, dst_row, jnp.zeros((16 - 2 * heads, width), BF16)])
    att_cols = jnp.pad(att_rows.T, ((0, 0), (0, 112)))

    shape = jax.ShapeDtypeStruct
    vmem = pltpu.VMEM
    square = shape((heads, nodes, nodes), BF16)
    output, input_grad, proj_grad, skip_grad, sums, _, _ = pl.pallas_call(
        functools.partial(layer_kernel, dims),
        out_shape=[
            shape((slots, rows, width), BF16),
            shape((slots, rows, width_in), BF16),
            shape((width_in, width), BF16),
            shape((width_in, width), BF16),
            shape((8, width), F32),
            square,
            square,
        ],
        in_specs=[ANY, ANY, ANY, SMEM, ANY, ANY, VMEM, VMEM, VMEM, VMEM, VMEM],
        out_specs=[ANY, ANY, ANY, ANY, VMEM, ANY, ANY],
        scratch_shapes=[
            vmem((nodes, width_in), BF16),
            vmem((nodes, width), BF16),
            vmem((nodes, max(nodes, 2 * width)), BF16),
            vmem((slots, rows, nodes), BF16),
            vmem((2, rows // 4, nodes), jnp.int32),
            vmem((width_in, width), BF16),
            vmem((width_in, width), BF16),
            vmem((nodes, width), F32),
            vmem((tallest, width), BF16),
            vmem((tallest, width), BF16),
            vmem((nodes, width), BF16),
            vmem((nodes, 128), F32),
            vmem((nodes, 128), BF16),
            vmem((16, nodes), F32),
            vmem((depth, rows, nodes), BF16),
            vmem((depth, rows, nodes), BF16),
            vmem((rows, nodes), BF16),
            vmem((2, nodes, rows), BF16),
            vmem((2, nodes, rows), BF16),
            vmem((8, width), F32),
            vmem((2, group, 8, width), F32),
            vmem((2, planes, 8, width), F32),
            vmem((4, width_in, quarter), BF16),
            vmem((4, chips, strip, quarter), BF16),
            vmem((4, planes) + piece, BF16),
            vmem((4, strip, quarter), BF16),
            dma((slots,)),
            dma((planes,)),
            dma((slots,)),
            dma((planes,)),
            dma((slots,)),
            dma((planes,)),
            dma((planes,)),
            dma((slots,)),
            dma((planes,)),
            dma((slots,)),
            dma((2, group)),
            dma((2, group)),
            dma((2, planes)),
            dma((2, planes)),
            dma((4, 6, max(chips, planes))),
            dma((4, 6, max(chips, planes))),
            dma((5,)),
            dma((2,)),
            dma((2,)),
            dma((4, 2)),
            dma((4,)),
        ],
        compiler_params=pltpu.CompilerParams(
            collective_id=0, has_side_effects=True, vmem_limit_bytes=63 * 2**20
        ),
    )(
        features,
        adjacency,
        cotangent,
        counts,
        proj_weight,
        skip_weight,
        att_rows,
        att_cols,
        attn_bias.reshape(1, width),
        norm_gain.reshape(1, width),
        norm_shift.reshape(1, width),
    )
    return (
        output,
        input_grad,
        proj_grad.astype(F32),
        skip_grad.astype(F32),
        sums[3].reshape(heads, head),
        sums[4].reshape(heads, head),
        sums[2],
        sums[0],
        sums[1],
    )


def solution(mesh):
    placed = (
        P("graph", "row", None),
        P("graph", "row", None),
        P("graph"),
        P(),
        P(),
        P(),
        P(),
        P(),
        P(),
        P(),
        P("graph", "row", None),
    )
    return jax.shard_map(
        functools.partial(shards, mesh.shape["row"], mesh.shape["graph"]),
        mesh=mesh,
        in_specs=placed,
        out_specs=(
            P("graph", "row", None),
            P("graph", "row", None),
            P(),
            P(),
            P(),
            P(),
            P(),
            P(),
            P(),
        ),
        check_vma=False,
    )
```

time: 874 us -> 293 us (0.34)
  waiting for transfers between devices: 466 us -> 0 us
  Pallas kernels: 0 us -> 276 us
  blocking collectives: 163 us -> 0 us
  matrix products: 106 us -> 0 us
  local copies, waits for them, and re-layouts: 65 us -> 8.34 us
  other arithmetic: 54.5 us -> 6.79 us
  between operations: 14.3 us -> 0.68 us
    pallas_call x0 -> x1, Pallas kernels: none -> 276 us  [shards(): pl.pallas_call(functools.partial(layer_kernel, dims), out_shape=[shape((s...]
    reduce_scatter x1 -> x0, waiting for transfers between devices: 211 us -> none  [shards(): lax.psum_scatter(source_grad, 'row', scatter_dimension=1, tiled=True)]
    psum x4 -> x0, blocking collectives: 163 us -> none  [the longest x1 43.4 us: shards(): lax.psum((proj_local, skip_local, dst_local, src_local, bias_local), ('gr...]
    psum x1 -> x0, waiting for transfers between devices: 124 us -> none  [shards(): lax.psum((proj_local, skip_local, dst_local, src_local, bias_local), ('gr...]
    all_gather x1 -> x0, waiting for transfers between devices: 115 us -> none  [shards(): gathered = lax.all_gather(hidden, 'row', axis=1, tiled=True)]
    dot_general x16 -> x0, matrix products: 68.4 us -> none  [the longest x3 16.2 us: attend(): jnp.einsum('hrn,nhc->rhc', shares, source.reshape(node_total, head_count,...]
    sub x3 -> x0, matrix products: 37.3 us -> none  [back_core(): grad_shares - spread]
    reduce_sum x8 -> x0, other arithmetic: 29.4 us -> none  [the longest x3 11.7 us: attend(): totals = jnp.sum(weight, axis=2) + (1.0 - live_row)[None, :]]
  transfers between devices with their start and end apart: 4 -> 0, of which waited for: 4 -> 0; matrix products, arithmetic and copies ran while one was open for 3% -> 0% of each run, Pallas kernels for 0% -> 0%
where the time goes in v2:
time: 293 us; the launch traced here: 292 us
  Pallas kernels  276 us (94%)
  local copies, waits for them, and re-layouts  8.34 us (3%)
  other arithmetic  6.79 us (2%)
    pallas_call x1, Pallas kernels, shards(): pl.pallas_call(functools.partial(layer_kernel, dims), out_shape=[shape((s...  276 us

profile of v2, /device:TPU:0, one launch (start us, length us, event | category | flops | bytes accessed | tf_op | source)
XLA Modules:
  0.0 292.3 jit_solution(8344828212547887662)
XLA Ops:
  0.7 0.1 pad.7.clone
  0.7 0.7 copy.24
  1.4 0.7 copy.23
  2.1 0.1 broadcast_bitcast_fusion
  2.2 0.1 maximum_maximum_fusion.att_rows
  2.3 0.0 copy-start.3
  2.3 0.2 copy.21
  2.5 0.8 pad.4.att_cols
  3.2 0.0 copy-done.3
  3.2 276.4 %shard_map.178 = (bf16[3,256,1024]{2,1,0:T(8,128)(2,1)}, bf16[3,256,1024]{2,1,0:T(8,128)(2,1)}, bf16[1024,1024]{1,0:T(8,128)(2,1)}, bf16[1024,1024]{1,0:T(8,128)...) custom-call(bf16[3,256,1024]{2,1,0:T(8,128)(2,1)} %feat.1, ...), custom_call_target="tpu_custom_call" | custom-call | tf_op jit(solution)/shard_map/pallas_call | solution.py:782
  279.7 1.6 fusion.1
  281.2 0.6 reshape_squeeze.6
  281.8 0.6 reshape_squeeze.7
  282.4 0.0 copy-start
  282.4 4.2 %convert_element_type.14 = f32[1024,1024]{1,0:T(8,128)} convert(bf16[1024,1024]{1,0:T(8,128)(2,1)} %get-tuple-element.16) | non-fusion elementwise | flops 1048576 | bytes 6291456 | tf_op jit(solution)/shard_map/convert_element_type | solution.py:863
  286.7 0.0 copy-done
  286.7 0.0 copy-start.2
  286.7 2.5 convert_element_type.15
  289.1 0.0 copy-done.2
  289.1 0.0 copy-start.1
  289.1 1.1 copy.27
  290.3 0.8 copy-done.1
  291.1 1.1 copy.28
  (4 shorter events, 0.0 us)
Async XLA Ops:
  2.3 0.9 copy-start.3
  282.4 4.2 %copy-start = (bf16[1024,1024]{1,0:T(8,128)(2,1)S(1)}, bf16[1024,1024]{1,0:T(8,128)(2,1)}, u32[]{:S(2)}) copy-start(bf16[1024,1024]{1,0:T(8,128)(2,1)} %get-tuple-element.17) | copy-start | bytes 6291460
  286.7 2.5 copy-start.2
  289.1 2.0 copy-start.1

commit v3 on v2

--- a/solution.py
+++ b/solution.py
@@ -14,6 +14,7 @@
 MASKED = -1e30
 TILE = 64
 WIDE_TILE = 256
+ROUNDS = 8
 F32 = jnp.float32
 BF16 = jnp.bfloat16
 ANY = pl.BlockSpec(memory_space=pl.ANY)
@@ -45,11 +46,6 @@
         return jnp.where(self.core == 1, turn, self.planes - 1 - turn)
 
 
-def elu_pair(value):
-    grown = jnp.exp(jnp.minimum(value, 0.0))
-    return jnp.where(value > 0, value, grown - 1.0), grown
-
-
 def sub_rows(index, size):
     return pl.ds(pl.multiple_of(index * size, size), size)
 
@@ -62,8 +58,8 @@
     counts,
     wp_in,
     ws_in,
-    att_rows,
-    att_cols,
+    att_dst_in,
+    att_src_in,
     bias,
     gain,
     shift,
@@ -74,6 +70,7 @@
     sums_out,
     p_all,
     q_all,
+    att_rows,
     feat_all,
     hid,
     wide,
@@ -132,6 +129,8 @@
     mask_all = wide.at[:, 0:nodes]
     back = wide.at[:, 0:width]
     stage = wide.at[:, width : 2 * width]
+    shared = wide.shape[1] < 3 * width
+    ig = stage if shared else wide.at[:, 2 * width : 3 * width]
 
     barrier = pltpu.get_barrier_semaphore()
     for k in range(1, planes):
@@ -216,6 +215,14 @@
         if i + 2 < len(loads):
             loads[i + 2].start()
 
+    row = lax.broadcasted_iota(jnp.int32, (16, head), 0)
+    for h in range(heads):
+        src_row, dst_row = (
+            kept[h : h + 1, :].astype(F32) for kept in (att_src_in, att_dst_in)
+        )
+        value = jnp.where(row == h, src_row, jnp.where(row == heads + h, dst_row, 0.0))
+        att_rows[:, h * head : (h + 1) * head] = value.astype(BF16)
+
     load_wp.wait()
     load_ws.wait()
     start(a_moves)
@@ -247,7 +254,7 @@
                 hid[here, part] = dot(value, wp[:, part]).astype(BF16)
                 pre[here, part] = dot(value, ws[:, part])
             made = hid[here, :]
-            dcol[here, :] = dot(made, att_cols[...]) * LOG2E
+            dcol[here, 0:16] = dot(made, att_rows[...], (1, 1)) * LOG2E
             srow[:, here] = dot(att_rows[...], made, (1, 1)) * LOG2E
 
         @pl.loop(0, planes)
@@ -308,21 +315,35 @@
     @pl.when(at.works)
     def _():
         def add_act(t, total):
-            act, _ = elu_pair(pre[sub_rows(t, tile), :])
+            here = sub_rows(t, tile)
+            value = pre[here, :]
+            act = jnp.where(value > 0, value, jnp.exp(jnp.minimum(value, 0.0)) - 1.0)
+            pre[here, :] = act
             return total + fold(act * live_of(t * tile, tile))
 
         number = jnp.maximum(live_count, 1).astype(F32)
         mean = total_of(lax.fori_loop(0, tiles, add_act, zero)) / number
 
         def add_square(t, total):
-            act, _ = elu_pair(pre[sub_rows(t, tile), :])
-            off = act - mean
+            off = pre[sub_rows(t, tile), :] - mean
             return total + fold(off * off * live_of(t * tile, tile))
 
-        stat[2:3, :] = total_of(lax.fori_loop(0, tiles, add_square, zero))
+        square = total_of(lax.fori_loop(0, tiles, add_square, zero))
+        for k in range(planes):
+            arrived(jnp.int32(k), *c_args)
+
+        def add_grad(t, totals):
+            here = sub_rows(t, tile)
+            grad = low[here, :].astype(F32) * live_of(t * tile, tile)
+            return totals[0] + fold(grad), totals[1] + fold(grad * (pre[here, :] - mean))
+
+        plain, along = lax.fori_loop(0, tiles, add_grad, (zero, zero))
         stat[0:1, :] = jnp.full((1, width), live_count.astype(F32))
         stat[1:2, :] = mean
-        stat[3:8, :] = jnp.zeros((5, width), F32)
+        stat[2:3, :] = square
+        stat[3:4, :] = total_of(plain)
+        stat[4:5, :] = total_of(along)
+        stat[5:8, :] = jnp.zeros((3, width), F32)
 
     @pl.when(jnp.logical_not(at.works))
     def _():
@@ -356,13 +377,17 @@
         number = sum(held[i, 0:1, :] for i in range(size))
         mean = sum(held[i, 0:1, :] * held[i, 1:2, :] for i in range(size))
         mean = mean / jnp.maximum(number, 1.0)
-        square = zero[0:1]
+        square, plain, along = zero[0:1], zero[0:1], zero[0:1]
         for i in range(size):
             off = held[i, 1:2, :] - mean
             square = square + held[i, 2:3, :] + held[i, 0:1, :] * off * off
+            plain = plain + held[i, 3:4, :]
+            along = along + held[i, 4:5, :] + held[i, 3:4, :] * off
         stat[0:1, :] = number
         stat[1:2, :] = mean
         stat[2:3, :] = square
+        stat[3:4, :] = plain
+        stat[4:5, :] = along
 
     def plain_sum(held, size):
         stat[...] = sum(held[i] for i in range(size))
@@ -381,47 +406,21 @@
         )
 
     norm_own = pltpu.make_async_copy(stage.at[block], out.at[at.slot], own_sem.at[3])
-    ig_own = pltpu.make_async_copy(stage.at[block], ig_out.at[at.slot], own_sem.at[4])
-
-    @pl.when(at.works)
-    def _():
-        @pl.loop(0, planes)
-        def _(k):
-            j = lax.rem(z + 1 + k, planes)
-
-            @pl.loop(0, rows // tile)
-            def _(t):
-                first = j * rows + t * tile
-                here = pl.ds(pl.multiple_of(first, tile), tile)
-                act, _ = elu_pair(pre[here, :])
-                normed = (act - mean) * inv_std
-                value = (gain[...] * normed + shift[...]) * live_of(first, tile)
-                stage[here, :] = value.astype(BF16)
-
-            pl.when(j != z)(give(out, n_send, n_recv, j).start)
-            pl.when(j == z)(norm_own.start)
-
-        for k in range(planes):
-            arrived(jnp.int32(k), *c_args)
-
-        def add_grad(t, totals):
-            here = sub_rows(t, tile)
-            act, _ = elu_pair(pre[here, :])
-            grad = low[here, :].astype(F32) * live_of(t * tile, tile)
-            return totals[0] + fold(grad), totals[1] + fold(grad * (act - mean))
-
-        plain, along = lax.fori_loop(0, tiles, add_grad, (zero, zero))
-        stat[0:1, :] = total_of(plain)
-        stat[1:2, :] = total_of(along)
-        stat[2:8, :] = jnp.zeros((6, width), F32)
-
-    @pl.when(jnp.logical_not(at.works))
-    def _():
-        stat[...] = zero
-
-    everywhere(1, plain_sum)
-    shift_grad = stat[0:1, :]
-    gain_grad = stat[1:2, :] * inv_std
+    ig_own = pltpu.make_async_copy(ig.at[block], ig_out.at[at.slot], own_sem.at[4])
+    bit_rows = rows // ROUNDS
+
+    def give_bit(r, to):
+        first = to * rows + r * bit_rows
+        return remote(
+            ig.at[pl.ds(pl.multiple_of(first, bit_rows), bit_rows)],
+            ig_out.at[at.slot, r * bit_rows : (r + 1) * bit_rows],
+            i_send.at[to, r],
+            i_recv.at[at.slot, r],
+            (g, to),
+        )
+
+    shift_grad = stat[3:4, :]
+    gain_grad = stat[4:5, :] * inv_std
     sums_out[0:1, :] = gain_grad
     sums_out[1:2, :] = shift_grad
     scale = gain[...] * inv_std
@@ -431,11 +430,14 @@
 
     @pl.when(at.works)
     def _():
-        def finish(t, total):
-            here = sub_rows(t, tile)
-            live = live_of(t * tile, tile)
-            act, grown = elu_pair(pre[here, :])
+        def finish(j, t, total):
+            first = j * rows + t * tile
+            here = pl.ds(pl.multiple_of(first, tile), tile)
+            live = live_of(first, tile)
+            act = pre[here, :]
+            grown = jnp.minimum(act, 0.0) + 1.0
             normed = (act - mean) * inv_std
+            stage[here, :] = ((gain[...] * normed + shift[...]) * live).astype(BF16)
             grad = low[here, :].astype(F32) * live
             grad = scale * (grad - shift_mean - normed * gain_mean) * live * grown
             grad_low = grad.astype(BF16)
@@ -460,7 +462,14 @@
             ).astype(BF16)
             return total + fold(grad)
 
-        stat[0:1, :] = total_of(lax.fori_loop(0, tiles, finish, zero))
+        def finish_block(k, total):
+            j = lax.rem(z + 1 + k, planes)
+            total = lax.fori_loop(0, rows // tile, functools.partial(finish, j), total)
+            pl.when(j != z)(give(out, n_send, n_recv, j).start)
+            pl.when(j == z)(norm_own.start)
+            return total
+
+        stat[0:1, :] = total_of(lax.fori_loop(0, planes, finish_block, zero))
         for h in range(depth):
             for copy in keep(h, block):
                 copy.wait()
@@ -471,10 +480,29 @@
     half_width = width // 2
     quarter = half_width // 2
     strip = width_in // chips
-    down = min(planes, strip // 16)
-    across = planes // down
     mine = pl.ds(pl.multiple_of(core * quarter, quarter), quarter)
     other = pl.ds(pl.multiple_of((1 - core) * quarter, quarter), quarter)
+    lines = planes.bit_length() - 1
+    regions = [(0, strip, 0, quarter)]
+    sides = []
+    for i in range(lines):
+        top, high, left, across = regions[-1]
+        bit = lax.rem(z // 2**i, 2)
+        pair = []
+        for b in (bit, 1 - bit):
+            if high >= 32:
+                pair.append((top + b * (high // 2), high // 2, left, across))
+            else:
+                pair.append((top, high, left + b * (across // 2), across // 2))
+        regions.append(pair[0])
+        sides.append((z + 2**i - 2 ** (i + 1) * bit, pair[0], pair[1]))
+
+    def cut(region):
+        top, high, left, across = region
+        return (
+            pl.ds(top if isinstance(top, int) else pl.multiple_of(top, high), high),
+            pl.ds(left if isinstance(left, int) else pl.multiple_of(left, across), across),
+        )
 
     def unit_of(u):
         kept = diff if u < 2 else mix
@@ -482,13 +510,6 @@
 
     def strip_of(index):
         return pl.ds(pl.multiple_of(index * strip, strip), strip)
-
-    def piece_of(index):
-        high, wide_piece = strip // down, quarter // across
-        return (
-            pl.ds(pl.multiple_of(lax.rem(index, down) * high, high), high),
-            pl.ds(pl.multiple_of(index // down * wide_piece, wide_piece), wide_piece),
-        )
 
     def to_core(u):
         return remote(
@@ -504,18 +525,17 @@
             (2 * peer + core, z),
         )
 
-    def to_line(u, peer, landed):
+    def to_line(u, i):
+        peer, kept, given = sides[i]
+        landing = line_in.at[u, i, 0 : kept[1], 0 : kept[3]]
         return remote(
-            line_out.at[u].at[piece_of(peer)],
-            line_in.at[u, landed],
-            r_send.at[u, 2, peer],
-            r_recv.at[u, 2, landed],
-            (g, peer),
-        )
-
-    def from_line(u, peer, landed):
-        where = swap.at[u].at[strip_of(chip)].at[piece_of(landed)]
-        return remote(where, where, r_send.at[u, 3, peer], r_recv.at[u, 3, landed], (g, peer))
+            line_out.at[u].at[cut(given)], landing, r_send.at[u, 2, i], r_recv.at[u, 2, i], (g, peer)
+        )
+
+    def from_line(u, i, landed=False):
+        peer, kept, given = sides[i]
+        where = swap.at[u].at[strip_of(chip)].at[cut(given if landed else kept)]
+        return remote(where, where, r_send.at[u, 3, i], r_recv.at[u, 3, i], (g, peer))
 
     def from_chip(u, peer, landed):
         where = swap.at[u].at[strip_of(landed)]
@@ -535,11 +555,13 @@
     def others(size, me):
         return [lax.rem(me + k, size) for k in range(1, size)]
 
+    last_step = 4 + 2 * lines
+
     def step(u, number):
         unit = unit_of(u)
         if number == 0:
             to_core(u).start()
-        if number == 1:
+        elif number == 1:
             to_core(u).wait()
 
             @pl.loop(0, width_in // tall)
@@ -550,36 +572,41 @@
 
             for peer in others(chips, chip):
                 to_chip(u, peer, chip).start()
-        if number == 2:
-            for peer in others(chips, chip):
-                to_chip(u, peer, peer).wait_recv()
-            value = unit[strip_of(chip), mine].astype(F32)
-            for peer in others(chips, chip):
-                value = value + plane_in[u, peer].astype(F32)
-            line_out[u] = value.astype(BF16)
-            for peer in others(planes, z):
-                to_line(u, peer, z).start()
-            for peer in others(chips, chip):
-                to_chip(u, peer, chip).wait_send()
-        if number == 3:
-            for peer in others(planes, z):
-                to_line(u, peer, peer).wait_recv()
-            value = line_out.at[u][piece_of(z)].astype(F32)
-            for peer in others(planes, z):
-                value = value + line_in[u, peer].astype(F32)
-            swap.at[u].at[strip_of(chip)][piece_of(z)] = value.astype(BF16)
-            for peer in others(planes, z):
-                from_line(u, peer, z).start()
-            for peer in others(planes, z):
-                to_line(u, peer, z).wait_send()
-        if number == 4:
-            for peer in others(planes, z):
-                from_line(u, peer, peer).wait_recv()
-            for peer in others(chips, chip):
-                from_chip(u, peer, chip).start()
-            for peer in others(planes, z):
-                from_line(u, peer, z).wait_send()
-        if number == 5:
+        elif number <= 2 + lines:
+            i = number - 3
+            if i < 0:
+                for peer in others(chips, chip):
+                    to_chip(u, peer, peer).wait_recv()
+                value = unit[strip_of(chip), mine].astype(F32)
+                for peer in others(chips, chip):
+                    value = value + plane_in[u, peer].astype(F32)
+                line_out[u] = value.astype(BF16)
+            else:
+                kept = sides[i][1]
+                to_line(u, i).wait_recv()
+                value = line_out.at[u][cut(kept)].astype(F32)
+                value = value + line_in[u, i, 0 : kept[1], 0 : kept[3]].astype(F32)
+                target = line_out.at[u] if i + 1 < lines else swap.at[u].at[strip_of(chip)]
+                target[cut(kept)] = value.astype(BF16)
+            if i + 1 < lines:
+                to_line(u, i + 1).start()
+            else:
+                from_line(u, lines - 1).start()
+            if i < 0:
+                for peer in others(chips, chip):
+                    to_chip(u, peer, chip).wait_send()
+            else:
+                to_line(u, i).wait_send()
+        elif number <= 2 + 2 * lines:
+            i = 2 + 2 * lines - number
+            from_line(u, i, True).wait_recv()
+            if i > 0:
+                from_line(u, i - 1).start()
+            else:
+                for peer in others(chips, chip):
+                    from_chip(u, peer, chip).start()
+            from_line(u, i).wait_send()
+        elif number < last_step:
             for peer in others(chips, chip):
                 from_chip(u, peer, peer).wait_recv()
             from_core(u, mine).start()
@@ -591,10 +618,14 @@
 
             for peer in others(chips, chip):
                 from_chip(u, peer, chip).wait_send()
-        if number == 6:
+        else:
             from_core(u, other).wait_recv()
             from_core(u, mine).wait_send()
             answer(u).start()
+
+    def steps(*work):
+        for u, number in work:
+            step(u, number)
 
     def answer(u):
         target = skip_out if u < 2 else proj_out
@@ -676,71 +707,90 @@
             back[here, part] = grad.astype(BF16)
             stat[1:2, part] += total_of(by_dst * own)
             stat[2:3, part] += total_of(by_src * own)
-        if turn == 1:
-            pl.when(j != z)(give(out, n_send, n_recv, j).wait_send)
-            pl.when(j == z)(norm_own.wait)
-            for f in range(width_in // head):
-                part = slice(f * head, (f + 1) * head)
-                stage[here, part] = (
-                    dot(back[here, :], wp[part, :], (1, 1)) + dot(low[here, :], ws[part, :], (1, 1))
-                ).astype(BF16)
-            pl.when(j != z)(give(ig_out, i_send, i_recv, j).start)
-            pl.when(j == z)(ig_own.start)
-
-    for turn in range(2):
-
+
+    def sent_norm(j):
+        pl.when(j != z)(give(out, n_send, n_recv, j).wait_send)
+        pl.when(j == z)(norm_own.wait)
+
+    def input_block(k):
+        j = lax.rem(z + 1 + k, planes)
+        here = sub_rows(j, rows)
+        if shared:
+            sent_norm(j)
+        for f in range(width_in // head):
+            part = slice(f * head, (f + 1) * head)
+            ig[here, part] = (
+                dot(back[here, :], wp[part, :], (1, 1)) + dot(low[here, :], ws[part, :], (1, 1))
+            ).astype(BF16)
+        pl.when(j == z)(ig_own.start)
+
+    def give_round(r):
+        @pl.when(at.works)
+        def _():
+            for peer in others(planes, z):
+                give_bit(r, peer).start()
+
+    def walk(turn, *work):
         @pl.loop(0, planes)
         def _(k):
             pl.when(at.works)(functools.partial(source_block, k, turn))
-            for when, work in PLAN[turn]:
-
-                @pl.when(k == when)
-                def _():
-                    for u, number in work:
-                        step(u, number)
-
-        product(2 + turn, back)
-        step(2 + turn, 0)
-
-    for u, number in PLAN[2]:
-        step(u, number)
-    everywhere(0, plain_sum)
+            for when, todo in work:
+                pl.when(k == when)(functools.partial(steps, *todo))
+
+    walk(0, (0, ((0, 1), (1, 1))), (3, ((0, 2), (1, 2))))
+    product(2, back)
+    step(2, 0)
+    walk(1, (0, ((2, 1),)), (3, ((2, 2),)))
+    product(3, back)
+    step(3, 0)
+
+    @pl.when(at.works)
+    def _():
+        pl.loop(0, planes)(input_block)
+
+    step(3, 1)
+    give_round(0)
+    exchange(1, group, g, stats_a, sa_send, sa_recv, lambda peer: (peer, z))
+    plain_sum(stats_a.at[1], group)
+    steps((0, 3), (1, 3))
+    for number in range(2, last_step + 1):
+        for u, ahead in ((3, 0), (2, 1), (0, 2), (1, 2)):
+            if number + ahead <= last_step:
+                step(u, number + ahead)
+        if number - 1 < ROUNDS:
+            give_round(number - 1)
+    for r in range(last_step, ROUNDS):
+        give_round(r)
+    exchange(1, planes, z, stats_b, sb_send, sb_recv, lambda peer: (g, peer))
+    plain_sum(stats_b.at[1], planes)
     sums_out[2:5, :] = stat[0:3, :]
     sums_out[5:8, :] = jnp.zeros((3, width), F32)
-    for u, number in PLAN[3]:
-        step(u, number)
 
     for s in range(slots):
-        for target, send, recv in ((out, n_send, n_recv), (ig_out, i_send, i_recv)):
-            pl.when(jnp.logical_not(at.mine[s]))(
-                remote(
-                    stage.at[sub_rows(0, rows)],
-                    target.at[s],
-                    send.at[0],
-                    recv.at[s],
-                    (g, at.owner(s)),
-                ).wait_recv
-            )
+
+        @pl.when(jnp.logical_not(at.mine[s]))
+        def _():
+            landing = out.at[s]
+            remote(landing, landing, n_send.at[0], n_recv.at[s], (g, at.owner(s))).wait_recv()
+            for r in range(ROUNDS):
+                landing = ig_out.at[s, r * bit_rows : (r + 1) * bit_rows]
+                remote(landing, landing, i_send.at[0, r], i_recv.at[s, r], (g, at.owner(s))).wait_recv()
 
     @pl.when(at.works)
     def _():
         ig_own.wait()
         for peer in others(planes, z):
-            give(ig_out, i_send, i_recv, peer).wait_send()
+            for r in range(ROUNDS):
+                give_bit(r, peer).wait_send()
+        if not shared:
+            for k in range(planes):
+                sent_norm(lax.rem(z + k, planes))
 
     for u in range(4):
         answer(u).wait()
     sent(f_moves)
     sent(a_moves)
     sent(c_moves)
-
-
-PLAN = (
-    ((0, ((0, 1),)), (1, ((1, 1),)), (3, ((0, 2), (1, 2)))),
-    ((0, ((2, 1),)), (1, ((0, 3), (1, 3))), (2, ((2, 2),)), (3, ((0, 4), (1, 4)))),
-    ((3, 1), (2, 3), (0, 5), (1, 5), (3, 2), (2, 4), (3, 3), (0, 6), (1, 6)),
-    ((2, 5), (3, 4), (2, 6), (3, 5), (3, 6)),
-)
 
 
 def shards(
@@ -766,15 +816,10 @@
     dma = pltpu.SemaphoreType.DMA
     chips = group // 2
     strip, quarter = width_in // chips, width // 4
-    down = min(planes, strip // 16)
-    piece = (strip // down, quarter // (planes // down))
+    lines = planes.bit_length() - 1
+    landing = (strip // 2, quarter) if strip >= 32 else (strip, quarter // 2)
     tallest = max(nodes, width_in)
     depth = 2 if nodes <= 1024 else 1
-
-    own = jnp.repeat(jnp.eye(heads, dtype=BF16), head, axis=1)
-    dst_row, src_row = own * attn_dst.reshape(1, width), own * attn_src.reshape(1, width)
-    att_rows = jnp.concatenate([src_row, dst_row, jnp.zeros((16 - 2 * heads, width), BF16)])
-    att_cols = jnp.pad(att_rows.T, ((0, 0), (0, 112)))
 
     shape = jax.ShapeDtypeStruct
     vmem = pltpu.VMEM
@@ -793,11 +838,12 @@
         in_specs=[ANY, ANY, ANY, SMEM, ANY, ANY, VMEM, VMEM, VMEM, VMEM, VMEM],
         out_specs=[ANY, ANY, ANY, ANY, VMEM, ANY, ANY],
         scratch_shapes=[
+            vmem((16, width), BF16),
             vmem((nodes, width_in), BF16),
             vmem((nodes, width), BF16),
-            vmem((nodes, max(nodes, 2 * width)), BF16),
+            vmem((nodes, max(nodes, (3 if nodes <= 1024 else 2) * width)), BF16),
             vmem((slots, rows, nodes), BF16),
-            vmem((2, rows // 4, nodes), jnp.int32),
+            vmem((2, max(rows // 4, TILE), nodes), jnp.int32),
             vmem((width_in, width), BF16),
             vmem((width_in, width), BF16),
             vmem((nodes, width), F32),
@@ -817,7 +863,7 @@
             vmem((2, planes, 8, width), F32),
             vmem((4, width_in, quarter), BF16),
             vmem((4, chips, strip, quarter), BF16),
-            vmem((4, planes) + piece, BF16),
+            vmem((4, lines) + landing, BF16),
             vmem((4, strip, quarter), BF16),
             dma((slots,)),
             dma((planes,)),
@@ -827,14 +873,14 @@
             dma((planes,)),
             dma((planes,)),
             dma((slots,)),
-            dma((planes,)),
-            dma((slots,)),
+            dma((planes, ROUNDS)),
+            dma((slots, ROUNDS)),
             dma((2, group)),
             dma((2, group)),
             dma((2, planes)),
             dma((2, planes)),
-            dma((4, 6, max(chips, planes))),
-            dma((4, 6, max(chips, planes))),
+            dma((4, 6, max(chips, lines))),
+            dma((4, 6, max(chips, lines))),
             dma((5,)),
             dma((2,)),
             dma((2,)),
@@ -851,8 +897,8 @@
         counts,
         proj_weight,
         skip_weight,
-        att_rows,
-        att_cols,
+        attn_dst,
+        attn_src,
         attn_bias.reshape(1, width),
         norm_gain.reshape(1, width),
         norm_shift.reshape(1, width),

time: 293 us -> 244 us (0.83)
  Pallas kernels: 276 us -> 230 us
    pallas_call x1, Pallas kernels: 276 us -> 230 us  [shards(): pl.pallas_call(functools.partial(layer_kernel, dims), out_shape=[shape((s...]
where the time goes in v3:
time: 244 us; the launch traced here: 243 us
  Pallas kernels  230 us (94%)
  other arithmetic  6.7 us (3%)
  local copies, waits for them, and re-layouts  5.88 us (2%)
    pallas_call x1, Pallas kernels, shards(): pl.pallas_call(functools.partial(layer_kernel, dims), out_shape=[shape((s...  230 us

profile of v3, /device:TPU:0, one launch (start us, length us, event | category | flops | bytes accessed | tf_op | source)
XLA Modules:
  0.0 243.0 jit_solution(13958265927917670019)
XLA Ops:
  0.6 229.8 %shard_map.178 = (bf16[3,256,1024]{2,1,0:T(8,128)(2,1)}, bf16[3,256,1024]{2,1,0:T(8,128)(2,1)}, bf16[1024,1024]{1,0:T(8,128)(2,1)}, bf16[1024,1024]{1,0:T(8,128)...) custom-call(bf16[3,256,1024]{2,1,0:T(8,128)(2,1)} %feat.1, ...), custom_call_target="tpu_custom_call" | custom-call | tf_op jit(solution)/shard_map/pallas_call | solution.py:827
  230.4 1.6 fusion
  232.0 0.6 reshape_squeeze.6
  232.6 0.6 reshape_squeeze.7
  233.2 0.0 copy-start
  233.2 4.2 %convert_element_type.6 = f32[1024,1024]{1,0:T(8,128)} convert(bf16[1024,1024]{1,0:T(8,128)(2,1)} %get-tuple-element.16) | non-fusion elementwise | flops 1048576 | bytes 6291456 | tf_op jit(solution)/shard_map/convert_element_type | solution.py:909
  237.4 0.0 copy-done
  237.4 0.0 copy-start.2
  237.4 2.5 %convert_element_type.7 = f32[1024,1024]{1,0:T(8,128)} convert(bf16[1024,1024]{1,0:T(8,128)(2,1)S(1)} %copy-done) | non-fusion elementwise | flops 1048576 | bytes 6291456 | tf_op jit(solution)/shard_map/convert_element_type | solution.py:910
  239.9 0.0 copy-done.2
  239.9 0.0 copy-start.1
  239.9 1.1 copy.22
  241.0 0.8 copy-done.1
  241.9 1.1 copy.23
Async XLA Ops:
  233.2 4.2 %copy-start = (bf16[1024,1024]{1,0:T(8,128)(2,1)S(1)}, bf16[1024,1024]{1,0:T(8,128)(2,1)}, u32[]{:S(2)}) copy-start(bf16[1024,1024]{1,0:T(8,128)(2,1)} %get-tuple-element.17) | copy-start | bytes 6291460
  237.4 2.5 %copy-start.2 = (bf16[3,256,1024]{2,1,0:T(8,128)(2,1)S(1)}, bf16[3,256,1024]{2,1,0:T(8,128)(2,1)}, u32[]{:S(2)}) copy-start(bf16[3,256,1024]{2,1,0:T(8,128)(2,1)} %get-tuple-element.35) | copy-start | bytes 4718596
  239.9 2.0 copy-start.1

commit v4 on v3

--- a/solution.py
+++ b/solution.py
@@ -15,6 +15,10 @@
 TILE = 64
 WIDE_TILE = 256
 ROUNDS = 8
+LOTS = 2
+PACE = 3
+BITS = 4
+EARLY = (0, 2, 3, 4, 5)
 F32 = jnp.float32
 BF16 = jnp.bfloat16
 ANY = pl.BlockSpec(memory_space=pl.ANY)
@@ -93,10 +97,18 @@
     stat,
     stats_a,
     stats_b,
-    swap,
-    plane_in,
-    line_in,
-    line_out,
+    swap_0,
+    swap_1,
+    swap_2,
+    plane_0,
+    plane_1,
+    plane_2,
+    line_in_0,
+    line_in_1,
+    line_in_2,
+    line_out_0,
+    line_out_1,
+    line_out_2,
     f_send,
     f_recv,
     a_send,
@@ -113,6 +125,7 @@
     sb_recv,
     r_send,
     r_recv,
+    lot_sem,
     own_sem,
     adj_sem,
     w_sem,
@@ -126,6 +139,7 @@
     at = Place(planes, slots, group)
     g, z = at.g, at.z
     block = sub_rows(z, rows)
+    resident = p_slot.shape[0] == heads
     mask_all = wide.at[:, 0:nodes]
     back = wide.at[:, 0:width]
     stage = wide.at[:, width : 2 * width]
@@ -163,36 +177,52 @@
             device_id_type=MESH,
         )
 
+    lot_rows = rows // LOTS
+
+    def lot_of(source, target, s, src, lot):
+        first = src * rows + lot * lot_rows
+        return (
+            source.at[s, lot * lot_rows : (lot + 1) * lot_rows],
+            target.at[pl.ds(pl.multiple_of(first, lot_rows), lot_rows)],
+        )
+
     def moves(source, target, send, recv, own):
         found = []
-        for s in range(slots):
-            to = at.owner(s)
-            away = remote(source.at[s], target.at[block], send.at[s], recv.at[z], (g, to))
-            local = pltpu.make_async_copy(source.at[s], target.at[block], own)
-            found.append((to, away, local))
+        for lot in range(LOTS):
+            for s in range(slots):
+                to = at.owner(s)
+                here, there = lot_of(source, target, s, z, lot)
+                away = remote(here, there, send.at[s, lot], recv.at[z, lot], (g, to))
+                local = pltpu.make_async_copy(here, there, own.at[lot])
+                found.append((to, away, local, lot))
         return found
 
     def start(copies):
-        for far in range(1, planes):
-            for to, away, _ in copies:
-                pl.when(jnp.abs(to - z) == far)(away.start)
-        for to, _, local in copies:
+        for lot in range(LOTS):
+            for far in range(1, planes):
+                for to, away, _, part in copies:
+                    if part == lot:
+                        pl.when(jnp.abs(to - z) == far)(away.start)
+        for to, _, local, _ in copies:
             pl.when(to == z)(local.start)
 
     def sent(copies):
-        for to, away, _ in copies:
+        for to, away, _, _ in copies:
             pl.when(to != z)(away.wait_send)
 
     def arrived(k, source, target, send, recv, own):
         src = lax.rem(z + k, planes)
-        there = target.at[sub_rows(src, rows)]
-        pl.when(k == 0)(pltpu.make_async_copy(source.at[0], there, own).wait)
-        pl.when(k != 0)(remote(source.at[0], there, send.at[0], recv.at[src], (g, src)).wait_recv)
+        for lot in range(LOTS):
+            here, there = lot_of(source, target, 0, src, lot)
+            pl.when(k == 0)(pltpu.make_async_copy(here, there, own.at[lot]).wait)
+            pl.when(k != 0)(
+                remote(here, there, send.at[0, lot], recv.at[src, lot], (g, src)).wait_recv
+            )
         return src
 
-    f_args = (feat, feat_all, f_send, f_recv, own_sem.at[0])
-    a_args = (mask_own, mask_all, a_send, a_recv, own_sem.at[1])
-    c_args = (cot, low, c_send, c_recv, own_sem.at[2])
+    f_args = (feat, feat_all, f_send, f_recv, lot_sem.at[0])
+    a_args = (mask_own, mask_all, a_send, a_recv, lot_sem.at[1])
+    c_args = (cot, low, c_send, c_recv, lot_sem.at[2])
     f_moves, a_moves, c_moves = moves(*f_args), moves(*a_args), moves(*c_args)
     start(f_moves)
 
@@ -236,6 +266,8 @@
     depth = p_slot.shape[0]
 
     def keep(h, here):
+        if resident:
+            return []
         slot = h % depth
         return [
             pltpu.make_async_copy(p_slot.at[slot], p_all.at[h, here], p_sem.at[0, slot]),
@@ -263,18 +295,21 @@
             here = sub_rows(src, rows)
             for h in range(heads):
                 part = slice(h * head, (h + 1) * head)
-                slot = h % depth
-
-                @pl.when((k > 0) | (h >= depth))
-                def _():
-                    for copy in keep(h, here):
-                        copy.wait()
+                slot = h if resident else h % depth
+                base = src * rows if resident else 0
+
+                if not resident:
+
+                    @pl.when((k > 0) | (h >= depth))
+                    def _():
+                        for copy in keep(h, here):
+                            copy.wait()
 
                 @pl.loop(0, rows // tall)
                 def _(t):
                     first = src * rows + t * tall
                     there = pl.ds(pl.multiple_of(first, tall), tall)
-                    inside = sub_rows(t, tall)
+                    inside = pl.ds(pl.multiple_of(base + t * tall, tall), tall)
                     masked = mask_all[there, :].astype(F32) + srow[h : h + 1, :]
                     dst = dcol[there, heads + h : heads + h + 1]
 
@@ -294,11 +329,11 @@
                     p_slot[slot, inside, :] = share.astype(BF16)
                     q_slot[slot, inside, :] = sloped.astype(BF16)
                     middle = jnp.sum(sloped, axis=1, keepdims=True)
-                    centered[inside, :] = (sloped - middle * share).astype(BF16)
+                    centered[sub_rows(t, tall), :] = (sloped - middle * share).astype(BF16)
 
                 for copy in keep(h, here):
                     copy.start()
-                mixed = dot(p_slot[slot], hid[:, part])
+                mixed = dot(p_slot[slot, sub_rows(src, rows) if resident else slice(None), :], hid[:, part])
                 mix[here, part] = mixed.astype(BF16)
                 pre[here, part] += mixed + bias[:, part]
                 diff[here, part] = dot(centered[...], hid[:, part]).astype(BF16)
@@ -396,14 +431,24 @@
     number, mean = stat[0:1, :], stat[1:2, :]
     inv_std = lax.rsqrt(stat[2:3, :] / number + EPSILON)
 
-    def give(target, send, recv, to):
+    tile_rows = rows // BITS
+
+    def give_norm(r, to):
+        first = to * rows + r * tile_rows
         return remote(
-            stage.at[sub_rows(to, rows)],
-            target.at[at.slot],
-            send.at[to],
-            recv.at[at.slot],
+            stage.at[pl.ds(pl.multiple_of(first, tile_rows), tile_rows)],
+            out.at[at.slot, r * tile_rows : (r + 1) * tile_rows],
+            n_send.at[to, r],
+            n_recv.at[at.slot, r],
             (g, to),
         )
+
+    def give_norms(first, last):
+        @pl.when(at.works)
+        def _():
+            for p in range(first, min(last, BITS * (planes - 1))):
+                r, k = p // (planes - 1), p % (planes - 1)
+                give_norm(r, lax.rem(z + 1 + k, planes)).start()
 
     norm_own = pltpu.make_async_copy(stage.at[block], out.at[at.slot], own_sem.at[3])
     ig_own = pltpu.make_async_copy(ig.at[block], ig_out.at[at.slot], own_sem.at[4])
@@ -430,8 +475,10 @@
 
     @pl.when(at.works)
     def _():
-        def finish(j, t, total):
-            first = j * rows + t * tile
+        def finish(r, t, total):
+            cut_rows = tile_rows // tile
+            j = lax.rem(z + 1 + t // cut_rows, planes)
+            first = j * rows + r * tile_rows + lax.rem(t, cut_rows) * tile
             here = pl.ds(pl.multiple_of(first, tile), tile)
             live = live_of(first, tile)
             act = pre[here, :]
@@ -462,14 +509,15 @@
             ).astype(BF16)
             return total + fold(grad)
 
-        def finish_block(k, total):
-            j = lax.rem(z + 1 + k, planes)
-            total = lax.fori_loop(0, rows // tile, functools.partial(finish, j), total)
-            pl.when(j != z)(give(out, n_send, n_recv, j).start)
-            pl.when(j == z)(norm_own.start)
-            return total
-
-        stat[0:1, :] = total_of(lax.fori_loop(0, planes, finish_block, zero))
+        total = zero
+        for r in range(BITS):
+            total = lax.fori_loop(
+                0, planes * tile_rows // tile, functools.partial(finish, r), total
+            )
+            for p in range(EARLY[r], EARLY[r + 1]):
+                give_norm(p // (planes - 1), lax.rem(z + 1 + p % (planes - 1), planes)).start()
+        norm_own.start()
+        stat[0:1, :] = total_of(total)
         for h in range(depth):
             for copy in keep(h, block):
                 copy.wait()
@@ -477,13 +525,17 @@
     chips = group // 2
     chip, core = g // 2, lax.rem(g, 2)
     partner = g + 1 - 2 * core
-    half_width = width // 2
-    quarter = half_width // 2
+    swaps, plane_ins = (swap_0, swap_1, swap_2), (plane_0, plane_1, plane_2)
+    line_ins, line_outs = (line_in_0, line_in_1, line_in_2), (line_out_0, line_out_1, line_out_2)
+    spans = ((0, width), (0, width // 2), (width // 2, width))
     strip = width_in // chips
-    mine = pl.ds(pl.multiple_of(core * quarter, quarter), quarter)
-    other = pl.ds(pl.multiple_of((1 - core) * quarter, quarter), quarter)
+
+    def share(u, which):
+        size = (spans[u][1] - spans[u][0]) // 2
+        return pl.ds(pl.multiple_of(which * size, size), size)
+
     lines = planes.bit_length() - 1
-    regions = [(0, strip, 0, quarter)]
+    regions = [(0, strip, 0, 2)]
     sides = []
     for i in range(lines):
         top, high, left, across = regions[-1]
@@ -497,56 +549,61 @@
         regions.append(pair[0])
         sides.append((z + 2**i - 2 ** (i + 1) * bit, pair[0], pair[1]))
 
-    def cut(region):
+    def cut(u, region):
         top, high, left, across = region
+        size = (spans[u][1] - spans[u][0]) // 4
+        left, across = left * size, across * size
         return (
             pl.ds(top if isinstance(top, int) else pl.multiple_of(top, high), high),
             pl.ds(left if isinstance(left, int) else pl.multiple_of(left, across), across),
         )
 
     def unit_of(u):
-        kept = diff if u < 2 else mix
-        return kept.at[0:width_in, u % 2 * half_width : (u % 2 + 1) * half_width]
+        kept = mix if u else diff
+        return kept.at[0:width_in, spans[u][0] : spans[u][1]]
 
     def strip_of(index):
         return pl.ds(pl.multiple_of(index * strip, strip), strip)
 
     def to_core(u):
         return remote(
-            unit_of(u).at[:, other], swap.at[u], r_send.at[u, 0, 0], r_recv.at[u, 0, 0], (partner, z)
+            unit_of(u).at[:, share(u, 1 - core)], swaps[u], r_send.at[u, 0, 0], r_recv.at[u, 0, 0], (partner, z)
         )
 
     def to_chip(u, peer, landed):
         return remote(
-            unit_of(u).at[strip_of(peer), mine],
-            plane_in.at[u, landed],
+            unit_of(u).at[strip_of(peer), share(u, core)],
+            plane_ins[u].at[landed],
             r_send.at[u, 1, peer],
             r_recv.at[u, 1, landed],
             (2 * peer + core, z),
         )
 
+    def landed_at(u, i):
+        _, high, _, across = sides[i][1]
+        return line_ins[u].at[i, 0:high, 0 : across * (spans[u][1] - spans[u][0]) // 4]
+
     def to_line(u, i):
         peer, kept, given = sides[i]
-        landing = line_in.at[u, i, 0 : kept[1], 0 : kept[3]]
         return remote(
-            line_out.at[u].at[cut(given)], landing, r_send.at[u, 2, i], r_recv.at[u, 2, i], (g, peer)
+            line_outs[u].at[cut(u, given)], landed_at(u, i), r_send.at[u, 2, i], r_recv.at[u, 2, i], (g, peer)
         )
 
     def from_line(u, i, landed=False):
         peer, kept, given = sides[i]
-        where = swap.at[u].at[strip_of(chip)].at[cut(given if landed else kept)]
+        where = swaps[u].at[strip_of(chip)].at[cut(u, given if landed else kept)]
         return remote(where, where, r_send.at[u, 3, i], r_recv.at[u, 3, i], (g, peer))
 
     def from_chip(u, peer, landed):
-        where = swap.at[u].at[strip_of(landed)]
+        where = swaps[u].at[strip_of(landed)]
         return remote(
             where, where, r_send.at[u, 4, peer], r_recv.at[u, 4, landed], (2 * peer + core, z)
         )
 
-    def from_core(u, columns):
+    def from_core(u, which):
         return remote(
-            swap.at[u],
-            unit_of(u).at[:, columns],
+            swaps[u],
+            unit_of(u).at[:, share(u, which)],
             r_send.at[u, 5, 0],
             r_recv.at[u, 5, 0],
             (partner, z),
@@ -558,7 +615,7 @@
     last_step = 4 + 2 * lines
 
     def step(u, number):
-        unit = unit_of(u)
+        unit, own = unit_of(u), share(u, core)
         if number == 0:
             to_core(u).start()
         elif number == 1:
@@ -567,8 +624,8 @@
             @pl.loop(0, width_in // tall)
             def _(t):
                 here = sub_rows(t, tall)
-                value = unit[here, mine].astype(F32) + swap[u, here, :].astype(F32)
-                unit[here, mine] = value.astype(BF16)
+                value = unit[here, own].astype(F32) + swaps[u][here, :].astype(F32)
+                unit[here, own] = value.astype(BF16)
 
             for peer in others(chips, chip):
                 to_chip(u, peer, chip).start()
@@ -577,17 +634,17 @@
             if i < 0:
                 for peer in others(chips, chip):
                     to_chip(u, peer, peer).wait_recv()
-                value = unit[strip_of(chip), mine].astype(F32)
+                value = unit[strip_of(chip), own].astype(F32)
                 for peer in others(chips, chip):
-                    value = value + plane_in[u, peer].astype(F32)
-                line_out[u] = value.astype(BF16)
+                    value = value + plane_ins[u][peer].astype(F32)
+                line_outs[u][...] = value.astype(BF16)
             else:
                 kept = sides[i][1]
                 to_line(u, i).wait_recv()
-                value = line_out.at[u][cut(kept)].astype(F32)
-                value = value + line_in[u, i, 0 : kept[1], 0 : kept[3]].astype(F32)
-                target = line_out.at[u] if i + 1 < lines else swap.at[u].at[strip_of(chip)]
-                target[cut(kept)] = value.astype(BF16)
+                value = line_outs[u][cut(u, kept)].astype(F32)
+                value = value + landed_at(u, i)[...].astype(F32)
+                target = line_outs[u] if i + 1 < lines else swaps[u].at[strip_of(chip)]
+                target[cut(u, kept)] = value.astype(BF16)
             if i + 1 < lines:
                 to_line(u, i + 1).start()
             else:
@@ -609,18 +666,18 @@
         elif number < last_step:
             for peer in others(chips, chip):
                 from_chip(u, peer, peer).wait_recv()
-            from_core(u, mine).start()
+            from_core(u, core).start()
 
             @pl.loop(0, width_in // tall)
             def _(t):
                 here = sub_rows(t, tall)
-                unit[here, mine] = swap[u, here, :]
+                unit[here, own] = swaps[u][here, :]
 
             for peer in others(chips, chip):
                 from_chip(u, peer, chip).wait_send()
         else:
-            from_core(u, other).wait_recv()
-            from_core(u, mine).wait_send()
+            from_core(u, 1 - core).wait_recv()
+            from_core(u, core).wait_send()
             answer(u).start()
 
     def steps(*work):
@@ -628,11 +685,12 @@
             step(u, number)
 
     def answer(u):
-        target = skip_out if u < 2 else proj_out
-        columns = slice(u % 2 * half_width, (u % 2 + 1) * half_width)
-        return pltpu.make_async_copy(unit_of(u), target.at[:, columns], out_sem.at[u])
+        target = proj_out if u else skip_out
+        return pltpu.make_async_copy(unit_of(u), target.at[:, slice(*spans[u])], out_sem.at[u])
 
     def fetch(j, h):
+        if resident:
+            return []
         place = pl.ds(pl.multiple_of(j * rows, rows), rows)
         slot = h % 2
         return [
@@ -642,7 +700,7 @@
 
     def product(u, right):
         unit = unit_of(u)
-        columns = slice(u % 2 * half_width, (u % 2 + 1) * half_width)
+        columns = slice(*spans[u])
 
         @pl.when(at.works)
         def _():
@@ -660,9 +718,8 @@
         for copy in fetch(lax.rem(z + 1, planes), 0):
             copy.start()
 
-    for u in (0, 1):
-        product(u, low)
-        step(u, 0)
+    product(0, low)
+    step(0, 0)
 
     def source_block(k, turn):
         j = lax.rem(z + 1 + k, planes)
@@ -690,9 +747,13 @@
 
             for copy in fetch(j, h):
                 copy.wait()
-            grad = dot(p_back[slot], low[:, part], (0, 0))
-            along = dot(q_back[slot], low[:, part], (0, 0))
-            spread = dot(q_back[slot], parts[...], (0, 0))
+            if resident:
+                p_now, q_now = p_slot[h, :, sub_rows(j, rows)], q_slot[h, :, sub_rows(j, rows)]
+            else:
+                p_now, q_now = p_back[slot], q_back[slot]
+            grad = dot(p_now, low[:, part], (0, 0))
+            along = dot(q_now, low[:, part], (0, 0))
+            spread = dot(q_now, parts[...], (0, 0))
             lane = lax.broadcasted_iota(jnp.int32, spread.shape, 1)
             chosen = (lane % heads == h) & (lane < 3 * heads)
             own = hid[here, part].astype(F32)
@@ -709,7 +770,11 @@
             stat[2:3, part] += total_of(by_src * own)
 
     def sent_norm(j):
-        pl.when(j != z)(give(out, n_send, n_recv, j).wait_send)
+        @pl.when(j != z)
+        def _():
+            for r in range(BITS):
+                give_norm(r, j).wait_send()
+
         pl.when(j == z)(norm_own.wait)
 
     def input_block(k):
@@ -724,43 +789,59 @@
             ).astype(BF16)
         pl.when(j == z)(ig_own.start)
 
-    def give_round(r):
+    def give_bits(first, last):
         @pl.when(at.works)
         def _():
-            for peer in others(planes, z):
-                give_bit(r, peer).start()
-
-    def walk(turn, *work):
+            for p in range(first, min(last, ROUNDS * (planes - 1))):
+                give_bit(p % ROUNDS, lax.rem(z + 1 + p // ROUNDS, planes)).start()
+
+    def S(u, number):
+        return lambda: step(u, number) if number <= last_step else None
+
+    def N(first, last):
+        return lambda: give_norms(first, last)
+
+    def R(first, last):
+        return lambda: give_bits(first, last)
+
+    def do(*work):
+        for one in work:
+            one()
+
+    def walk(turn, **work):
         @pl.loop(0, planes)
         def _(k):
             pl.when(at.works)(functools.partial(source_block, k, turn))
-            for when, todo in work:
-                pl.when(k == when)(functools.partial(steps, *todo))
-
-    walk(0, (0, ((0, 1), (1, 1))), (3, ((0, 2), (1, 2))))
+            for when, todo in work.items():
+                pl.when(k == int(when[1:]))(functools.partial(do, *todo))
+
+    def input_of(k):
+        pl.when(at.works)(functools.partial(input_block, k))
+
+    def I(k):
+        return lambda: input_of(k)
+
+    last = BITS * (planes - 1)
+    do(N(5, 7))
+    walk(0, k0=(S(0, 1),), k1=(N(7, 8),), k3=(N(8, 9),))
+    product(1, back)
+    do(S(1, 0), N(9, 10))
+    walk(1, k0=(S(1, 1), N(10, 11)), k1=(I(0), N(11, last)), k3=(S(0, 2), R(0, 0)))
     product(2, back)
-    step(2, 0)
-    walk(1, (0, ((2, 1),)), (3, ((2, 2),)))
-    product(3, back)
-    step(3, 0)
-
-    @pl.when(at.works)
-    def _():
-        pl.loop(0, planes)(input_block)
-
-    step(3, 1)
-    give_round(0)
+    do(S(2, 0), R(0, 0), I(1), S(2, 1), S(0, 3), I(2), S(1, 2), R(0, 6))
+    for k in range(3, planes):
+        input_of(k)
     exchange(1, group, g, stats_a, sa_send, sa_recv, lambda peer: (peer, z))
     plain_sum(stats_a.at[1], group)
-    steps((0, 3), (1, 3))
+    done, given = [3, 2, 1], 6
     for number in range(2, last_step + 1):
-        for u, ahead in ((3, 0), (2, 1), (0, 2), (1, 2)):
-            if number + ahead <= last_step:
-                step(u, number + ahead)
-        if number - 1 < ROUNDS:
-            give_round(number - 1)
-    for r in range(last_step, ROUNDS):
-        give_round(r)
+        for u, target in ((2, number), (1, number + 1), (0, number + 2)):
+            while done[u] < min(target, last_step):
+                done[u] += 1
+                step(u, done[u])
+        give_bits(given, given + PACE)
+        given += PACE
+    give_bits(given, ROUNDS * (planes - 1))
     exchange(1, planes, z, stats_b, sb_send, sb_recv, lambda peer: (g, peer))
     plain_sum(stats_b.at[1], planes)
     sums_out[2:5, :] = stat[0:3, :]
@@ -770,8 +851,9 @@
 
         @pl.when(jnp.logical_not(at.mine[s]))
         def _():
-            landing = out.at[s]
-            remote(landing, landing, n_send.at[0], n_recv.at[s], (g, at.owner(s))).wait_recv()
+            for r in range(BITS):
+                landing = out.at[s, r * tile_rows : (r + 1) * tile_rows]
+                remote(landing, landing, n_send.at[0, r], n_recv.at[s, r], (g, at.owner(s))).wait_recv()
             for r in range(ROUNDS):
                 landing = ig_out.at[s, r * bit_rows : (r + 1) * bit_rows]
                 remote(landing, landing, i_send.at[0, r], i_recv.at[s, r], (g, at.owner(s))).wait_recv()
@@ -786,11 +868,74 @@
             for k in range(planes):
                 sent_norm(lax.rem(z + k, planes))
 
-    for u in range(4):
+    for u in range(3):
         answer(u).wait()
     sent(f_moves)
     sent(a_moves)
     sent(c_moves)
+
+
+def finish_kernel(
+    out_in,
+    ig_in,
+    proj_in,
+    skip_in,
+    sums,
+    out,
+    ig,
+    proj,
+    skip,
+    att_dst,
+    att_src,
+    bias,
+    gain,
+    shift,
+    narrow,
+    full,
+    held,
+    copy_sem,
+    in_sem,
+    wide_sem,
+):
+    heads, head = att_dst.shape
+    passing = [
+        (
+            pltpu.make_async_copy(source.at[s], held.at[i, s], copy_sem.at[i, s]),
+            pltpu.make_async_copy(held.at[i, s], target.at[s], copy_sem.at[i, s]),
+        )
+        for i, (source, target) in enumerate(((out_in, out), (ig_in, ig)))
+        for s in range(out.shape[0])
+    ]
+    size = proj.shape[0] // 4
+    lots = []
+    for i, (source, target) in enumerate(((proj_in, proj), (skip_in, skip))):
+        for k in range(4):
+            rows = pl.ds(k * size, size)
+            load = pltpu.make_async_copy(source.at[rows], narrow.at[i, rows], in_sem.at[i, k])
+            store = pltpu.make_async_copy(full.at[i, rows], target.at[rows], wide_sem.at[i, k])
+            lots.append((i, rows, load, store))
+    for _, _, load, _ in lots:
+        load.start()
+    for load, _ in passing:
+        load.start()
+    for h in range(heads):
+        part = slice(h * head, (h + 1) * head)
+        att_dst[h : h + 1, :] = sums[3:4, part]
+        att_src[h : h + 1, :] = sums[4:5, part]
+    gain[...] = sums[0:1, :]
+    shift[...] = sums[1:2, :]
+    bias[...] = sums[2:3, :]
+    for i, rows, load, store in lots:
+        load.wait()
+        full[i, rows, :] = narrow[i, rows, :].astype(F32)
+        store.start()
+    for load, store in passing:
+        load.wait()
+        store.start()
+    for _, _, _, store in lots:
+        store.wait()
+    for _, store in passing:
+        store.wait()
 
 
 def shards(
@@ -815,15 +960,15 @@
     dims = (planes, group, slots, rows, nodes, heads, head, width_in)
     dma = pltpu.SemaphoreType.DMA
     chips = group // 2
-    strip, quarter = width_in // chips, width // 4
+    strip, shares = width_in // chips, (width // 2, width // 4, width // 4)
     lines = planes.bit_length() - 1
-    landing = (strip // 2, quarter) if strip >= 32 else (strip, quarter // 2)
     tallest = max(nodes, width_in)
-    depth = 2 if nodes <= 1024 else 1
+    resident = nodes <= 1024
+    kept = (heads, nodes, nodes) if resident else (1, rows, nodes)
 
     shape = jax.ShapeDtypeStruct
     vmem = pltpu.VMEM
-    square = shape((heads, nodes, nodes), BF16)
+    square = shape((heads, 16, 128) if resident else (heads, nodes, nodes), BF16)
     output, input_grad, proj_grad, skip_grad, sums, _, _ = pl.pallas_call(
         functools.partial(layer_kernel, dims),
         out_shape=[
@@ -853,39 +998,40 @@
             vmem((nodes, 128), F32),
             vmem((nodes, 128), BF16),
             vmem((16, nodes), F32),
-            vmem((depth, rows, nodes), BF16),
-            vmem((depth, rows, nodes), BF16),
+            vmem(kept, BF16),
+            vmem(kept, BF16),
             vmem((rows, nodes), BF16),
-            vmem((2, nodes, rows), BF16),
-            vmem((2, nodes, rows), BF16),
+            vmem((1 if resident else 2, 16 if resident else nodes, rows), BF16),
+            vmem((1 if resident else 2, 16 if resident else nodes, rows), BF16),
             vmem((8, width), F32),
             vmem((2, group, 8, width), F32),
             vmem((2, planes, 8, width), F32),
-            vmem((4, width_in, quarter), BF16),
-            vmem((4, chips, strip, quarter), BF16),
-            vmem((4, lines) + landing, BF16),
-            vmem((4, strip, quarter), BF16),
-            dma((slots,)),
-            dma((planes,)),
-            dma((slots,)),
-            dma((planes,)),
-            dma((slots,)),
-            dma((planes,)),
-            dma((planes,)),
-            dma((slots,)),
+            *(vmem((width_in, one), BF16) for one in shares),
+            *(vmem((chips, strip, one), BF16) for one in shares),
+            *(vmem((lines, max(strip // 2, 16), one), BF16) for one in shares),
+            *(vmem((strip, one), BF16) for one in shares),
+            dma((slots, LOTS)),
+            dma((planes, LOTS)),
+            dma((slots, LOTS)),
+            dma((planes, LOTS)),
+            dma((slots, LOTS)),
+            dma((planes, LOTS)),
+            dma((planes, BITS)),
+            dma((slots, BITS)),
             dma((planes, ROUNDS)),
             dma((slots, ROUNDS)),
             dma((2, group)),
             dma((2, group)),
             dma((2, planes)),
             dma((2, planes)),
-            dma((4, 6, max(chips, lines))),
-            dma((4, 6, max(chips, lines))),
+            dma((3, 6, max(chips, lines))),
+            dma((3, 6, max(chips, lines))),
+            dma((3, LOTS)),
             dma((5,)),
             dma((2,)),
             dma((2,)),
             dma((4, 2)),
-            dma((4,)),
+            dma((3,)),
         ],
         compiler_params=pltpu.CompilerParams(
             collective_id=0, has_side_effects=True, vmem_limit_bytes=63 * 2**20
@@ -903,16 +1049,44 @@
         norm_gain.reshape(1, width),
         norm_shift.reshape(1, width),
     )
+    line = shape((1, width), F32)
+    weight, att = shape((width_in, width), F32), shape((heads, head), F32)
+    output, input_grad, proj_grad, skip_grad, dst_grad, src_grad, bias, gain, shift = pl.pallas_call(
+        finish_kernel,
+        out_shape=[
+            shape(output.shape, BF16),
+            shape(input_grad.shape, BF16),
+            weight,
+            weight,
+            att,
+            att,
+            line,
+            line,
+            line,
+        ],
+        in_specs=[ANY] * 4 + [VMEM],
+        out_specs=[ANY] * 4 + [VMEM] * 5,
+        scratch_shapes=[
+            vmem((2, width_in, width), BF16),
+            vmem((2, width_in, width), F32),
+            vmem((2,) + output.shape, BF16),
+            dma((2, slots)),
+            dma((2, 4)),
+            dma((2, 4)),
+        ],
+        compiler_params=pltpu.CompilerParams(vmem_limit_bytes=60 * 2**20),
+    )(output, input_grad, proj_grad, skip_grad, sums)
+    flat = (width,)
     return (
         output,
         input_grad,
-        proj_grad.astype(F32),
-        skip_grad.astype(F32),
-        sums[3].reshape(heads, head),
-        sums[4].reshape(heads, head),
-        sums[2],
-        sums[0],
-        sums[1],
+        proj_grad,
+        skip_grad,
+        dst_grad,
+        src_grad,
+        bias.reshape(flat),
+        gain.reshape(flat),
+        shift.reshape(flat),
     )
 
 

time: 244 us -> 228 us (0.934)
  other arithmetic: 6.7 us -> 0 us
  local copies, waits for them, and re-layouts: 5.88 us -> 0 us
  Pallas kernels: 230 us -> 227 us
    pallas_call x1, Pallas kernels: 230 us -> 218 us  [shards(): pl.pallas_call(functools.partial(layer_kernel, dims), out_shape=[shape((s...]
    pallas_call x0 -> x1, Pallas kernels: none -> 8.76 us  [shards(): pl.pallas_call(finish_kernel, out_shape=[shape(output.shape, BF16), shape...]
    convert_element_type x2 -> x0, other arithmetic: 6.7 us -> none  [the longest x1 4.22 us: shards(): proj_grad.astype(F32)]
    unnamed x8 -> x0, local copies, waits for them, and re-layouts: 3.12 us -> none
where the time goes in v4:
time: 228 us; the launch traced here: 227 us
  Pallas kernels  227 us (100%)
    pallas_call x1, Pallas kernels, shards(): pl.pallas_call(functools.partial(layer_kernel, dims), out_shape=[shape((s...  218 us
    pallas_call x1, Pallas kernels, shards(): pl.pallas_call(finish_kernel, out_shape=[shape(output.shape, BF16), shape...  8.76 us

profile of v4, /device:TPU:0, one launch (start us, length us, event | category | flops | bytes accessed | tf_op | source)
XLA Modules:
  0.0 227.3 jit_solution(16750068562672810634)
XLA Ops:
  0.6 217.8 %shard_map.178 = (bf16[3,256,1024]{2,1,0:T(8,128)(2,1)}, bf16[3,256,1024]{2,1,0:T(8,128)(2,1)}, bf16[1024,1024]{1,0:T(8,128)(2,1)}, bf16[1024,1024]{1,0:T(8,128)...) custom-call(bf16[3,256,1024]{2,1,0:T(8,128)(2,1)} %feat.1, ...), custom_call_target="tpu_custom_call" | custom-call | tf_op jit(solution)/shard_map/pallas_call | solution.py:972
  218.4 8.8 %shard_map.179 = (bf16[3,256,1024]{2,1,0:T(8,128)(2,1)}, bf16[3,256,1024]{2,1,0:T(8,128)(2,1)}, f32[1024,1024]{1,0:T(8,128)}, f32[1024,1024]{1,0:T(8,128)}, f32[...) custom-call(bf16[3,256,1024]{2,1,0:T(8,128)(2,1)} %get-tuple-element.23.out_i, ...), custom_call_target="tpu_custom_call" | custom-call | tf_op jit(solution)/shard_map/pallas_call | solution.py:1054

commit v5 on v4

--- a/solution.py
+++ b/solution.py
@@ -876,6 +876,7 @@
 
 
 def finish_kernel(
+    near,
     out_in,
     ig_in,
     proj_in,
@@ -898,26 +899,29 @@
     wide_sem,
 ):
     heads, head = att_dst.shape
-    passing = [
-        (
-            pltpu.make_async_copy(source.at[s], held.at[i, s], copy_sem.at[i, s]),
-            pltpu.make_async_copy(held.at[i, s], target.at[s], copy_sem.at[i, s]),
-        )
-        for i, (source, target) in enumerate(((out_in, out), (ig_in, ig)))
-        for s in range(out.shape[0])
-    ]
+    passing = []
+    for i, (source, target) in enumerate(((out_in, out), (ig_in, ig))):
+        for s in range(out.shape[0]):
+            load = None if near else pltpu.make_async_copy(source.at[s], held.at[i, s], copy_sem.at[i, s])
+            kept = source.at[s] if near else held.at[i, s]
+            store = pltpu.make_async_copy(kept, target.at[s], copy_sem.at[i, s])
+            passing.append((load, store))
     size = proj.shape[0] // 4
     lots = []
     for i, (source, target) in enumerate(((proj_in, proj), (skip_in, skip))):
         for k in range(4):
             rows = pl.ds(k * size, size)
-            load = pltpu.make_async_copy(source.at[rows], narrow.at[i, rows], in_sem.at[i, k])
+            load = None if near else pltpu.make_async_copy(source.at[rows], narrow.at[i, rows], in_sem.at[i, k])
             store = pltpu.make_async_copy(full.at[i, rows], target.at[rows], wide_sem.at[i, k])
-            lots.append((i, rows, load, store))
-    for _, _, load, _ in lots:
-        load.start()
-    for load, _ in passing:
-        load.start()
+            lots.append((source if near else narrow.at[i], i, rows, load, store))
+    if near:
+        for _, store in passing:
+            store.start()
+    else:
+        for _, _, _, load, _ in lots:
+            load.start()
+        for load, _ in passing:
+            load.start()
     for h in range(heads):
         part = slice(h * head, (h + 1) * head)
         att_dst[h : h + 1, :] = sums[3:4, part]
@@ -925,14 +929,16 @@
     gain[...] = sums[0:1, :]
     shift[...] = sums[1:2, :]
     bias[...] = sums[2:3, :]
-    for i, rows, load, store in lots:
-        load.wait()
-        full[i, rows, :] = narrow[i, rows, :].astype(F32)
+    for source, i, rows, load, store in lots:
+        if not near:
+            load.wait()
+        full[i, rows, :] = source[rows, :].astype(F32)
         store.start()
-    for load, store in passing:
-        load.wait()
-        store.start()
-    for _, _, _, store in lots:
+    if not near:
+        for load, store in passing:
+            load.wait()
+            store.start()
+    for _, _, _, _, store in lots:
         store.wait()
     for _, store in passing:
         store.wait()
@@ -968,14 +974,15 @@
 
     shape = jax.ShapeDtypeStruct
     vmem = pltpu.VMEM
+    near = pltpu.VMEM if resident else shape
     square = shape((heads, 16, 128) if resident else (heads, nodes, nodes), BF16)
     output, input_grad, proj_grad, skip_grad, sums, _, _ = pl.pallas_call(
         functools.partial(layer_kernel, dims),
         out_shape=[
-            shape((slots, rows, width), BF16),
-            shape((slots, rows, width_in), BF16),
-            shape((width_in, width), BF16),
-            shape((width_in, width), BF16),
+            near((slots, rows, width), BF16),
+            near((slots, rows, width_in), BF16),
+            near((width_in, width), BF16),
+            near((width_in, width), BF16),
             shape((8, width), F32),
             square,
             square,
@@ -1034,7 +1041,9 @@
             dma((3,)),
         ],
         compiler_params=pltpu.CompilerParams(
-            collective_id=0, has_side_effects=True, vmem_limit_bytes=63 * 2**20
+            collective_id=0,
+            has_side_effects=True,
+            vmem_limit_bytes=(54 if resident else 63) * 2**20,
         ),
     )(
         features,
@@ -1052,7 +1061,7 @@
     line = shape((1, width), F32)
     weight, att = shape((width_in, width), F32), shape((heads, head), F32)
     output, input_grad, proj_grad, skip_grad, dst_grad, src_grad, bias, gain, shift = pl.pallas_call(
-        finish_kernel,
+        functools.partial(finish_kernel, resident),
         out_shape=[
             shape(output.shape, BF16),
             shape(input_grad.shape, BF16),
@@ -1064,17 +1073,17 @@
             line,
             line,
         ],
-        in_specs=[ANY] * 4 + [VMEM],
+        in_specs=[VMEM if resident else ANY] * 4 + [VMEM],
         out_specs=[ANY] * 4 + [VMEM] * 5,
         scratch_shapes=[
-            vmem((2, width_in, width), BF16),
+            vmem((1, 16, 128) if resident else (2, width_in, width), BF16),
             vmem((2, width_in, width), F32),
-            vmem((2,) + output.shape, BF16),
+            vmem((2, slots, 16, 128) if resident else (2,) + output.shape, BF16),
             dma((2, slots)),
             dma((2, 4)),
             dma((2, 4)),
         ],
-        compiler_params=pltpu.CompilerParams(vmem_limit_bytes=60 * 2**20),
+        compiler_params=pltpu.CompilerParams(vmem_limit_bytes=(40 if resident else 60) * 2**20),
     )(output, input_grad, proj_grad, skip_grad, sums)
     flat = (width,)
     return (

time: 228 us -> 225 us (0.987)
  Pallas kernels: 227 us -> 223 us
    pallas_call x2, Pallas kernels: 227 us -> 223 us  [the longest x1 218 us: shards(): pl.pallas_call(functools.partial(layer_kernel, dims), out_shape=[near((sl...]
where the time goes in v5:
time: 225 us; the launch traced here: 224 us
  Pallas kernels  223 us (99%)
    pallas_call x1, Pallas kernels, shards(): pl.pallas_call(functools.partial(layer_kernel, dims), out_shape=[near((sl...  218 us
    pallas_call x1, Pallas kernels, shards(): pl.pallas_call(functools.partial(finish_kernel, resident), out_shape=[sha...  5.05 us

profile of v5, /device:TPU:0, one launch (start us, length us, event | category | flops | bytes accessed | tf_op | source)
XLA Modules:
  0.0 224.5 jit_solution(17946874485879597190)
XLA Ops:
  0.6 217.8 %shard_map.178 = (bf16[3,256,1024]{2,1,0:T(8,128)(2,1)S(1)}, bf16[3,256,1024]{2,1,0:T(8,128)(2,1)S(1)}, bf16[1024,1024]{1,0:T(8,128)(2,1)S(1)}, bf16[1024,1024]{...) custom-call(bf16[3,256,1024]{2,1,0:T(8,128)(2,1)} %feat.1, ...), custom_call_target="tpu_custom_call" | custom-call | tf_op jit(solution)/shard_map/pallas_call | solution.py:979
  218.5 0.0 copy-start
  218.5 0.7 copy-done
  219.3 5.1 %shard_map.179 = (bf16[3,256,1024]{2,1,0:T(8,128)(2,1)}, bf16[3,256,1024]{2,1,0:T(8,128)(2,1)}, f32[1024,1024]{1,0:T(8,128)}, f32[1024,1024]{1,0:T(8,128)}, f32[...) custom-call(bf16[3,256,1024]{2,1,0:T(8,128)(2,1)S(1)} %get-tuple-element.23.o, ...), custom_call_target="tpu_custom_call" | custom-call | tf_op jit(solution)/shard_map/pallas_call | solution.py:1063
Async XLA Ops:
  218.5 0.8 copy-start

commit v6 on v5

--- a/solution.py
+++ b/solution.py
@@ -18,7 +18,7 @@
 LOTS = 2
 PACE = 3
 BITS = 4
-EARLY = (0, 2, 3, 4, 5)
+EARLY = (0, 3, 5, 6, 7)
 F32 = jnp.float32
 BF16 = jnp.bfloat16
 ANY = pl.BlockSpec(memory_space=pl.ANY)
@@ -822,13 +822,13 @@
         return lambda: input_of(k)
 
     last = BITS * (planes - 1)
-    do(N(5, 7))
-    walk(0, k0=(S(0, 1),), k1=(N(7, 8),), k3=(N(8, 9),))
+    do(N(7, 8))
+    walk(0, k0=(S(0, 1),), k1=(N(8, 9),), k3=(N(9, 10),))
     product(1, back)
-    do(S(1, 0), N(9, 10))
-    walk(1, k0=(S(1, 1), N(10, 11)), k1=(I(0), N(11, last)), k3=(S(0, 2), R(0, 0)))
+    do(S(1, 0), N(10, 11))
+    walk(1, k0=(S(1, 1), N(11, last)), k1=(I(0),), k3=(S(0, 2), R(0, 0)))
     product(2, back)
-    do(S(2, 0), R(0, 0), I(1), S(2, 1), S(0, 3), I(2), S(1, 2), R(0, 6))
+    do(S(2, 0), R(0, 0), I(1), S(2, 1), S(0, 3), R(0, 3), I(2), S(1, 2), R(3, 6))
     for k in range(3, planes):
         input_of(k)
     exchange(1, group, g, stats_a, sa_send, sa_recv, lambda peer: (peer, z))

time: 225 us -> 225 us (level)
  no operation moved by 1% of the time
where the time goes in v6:
time: 225 us
  Pallas kernels  223 us (99%)
    pallas_call x1, Pallas kernels, shards(): pl.pallas_call(functools.partial(layer_kernel, dims), out_shape=[near((sl...  218 us
    pallas_call x1, Pallas kernels, shards(): pl.pallas_call(functools.partial(finish_kernel, resident), out_shape=[sha...  5.05 us

profile of v6, /device:TPU:0, one launch (start us, length us, event | category | flops | bytes accessed | tf_op | source)
XLA Modules:
  0.0 224.5 jit_solution(11230689428573601870)
XLA Ops:
  0.6 217.9 %shard_map.178 = (bf16[3,256,1024]{2,1,0:T(8,128)(2,1)S(1)}, bf16[3,256,1024]{2,1,0:T(8,128)(2,1)S(1)}, bf16[1024,1024]{1,0:T(8,128)(2,1)S(1)}, bf16[1024,1024]{...) custom-call(bf16[3,256,1024]{2,1,0:T(8,128)(2,1)} %feat.1, ...), custom_call_target="tpu_custom_call" | custom-call | tf_op jit(solution)/shard_map/pallas_call | solution.py:979
  218.5 0.0 copy-start
  218.5 0.7 copy-done
  219.3 5.1 %shard_map.179 = (bf16[3,256,1024]{2,1,0:T(8,128)(2,1)}, bf16[3,256,1024]{2,1,0:T(8,128)(2,1)}, f32[1024,1024]{1,0:T(8,128)}, f32[1024,1024]{1,0:T(8,128)}, f32[...) custom-call(bf16[3,256,1024]{2,1,0:T(8,128)(2,1)S(1)} %get-tuple-element.23.o, ...), custom_call_target="tpu_custom_call" | custom-call | tf_op jit(solution)/shard_map/pallas_call | solution.py:1063
Async XLA Ops:
  218.5 0.8 copy-start
